TPU v7x, 32 devices: a whole 2x2x4 slice. The times are simulated.
32 devices in a mesh: dp: 4 (over y, x), expert: 8 (over z, core).
Axes of the slice: x: 2, y: 2, z: 4, core: 2. Of those that a mesh axis runs over, the one named last changes fastest.
Arguments:
- tokens: bfloat16 [4096, 2048], P(('dp', 'expert')), may hold values from -6 to 6
- cotangent: bfloat16 [4096, 2048], P(('dp', 'expert')), may hold values from -6 to 6
- expert_ids: int32 [4096, 4], P(('dp', 'expert')), may hold values from 0 to 7, all different within a row; in each aligned block of 128 rows (0 to 127, 128 to 255, ...) at most 96 rows name the same one
- gate_probs: bfloat16 [4096, 4], P(('dp', 'expert')), may hold values from 0.049804688 to 0.5
- w_in: bfloat16 [8, 2048, 1536], P('expert', 'dp'), may hold values from -0.125 to 0.125
- w_out: bfloat16 [8, 768, 2048], P('expert', 'dp'), may hold values from -0.21875 to 0.21875
- mom_in: float32 [8, 2048, 1536], P('expert', 'dp'), may hold values from -12 to 12
- mom_out: float32 [8, 768, 2048], P('expert', 'dp'), may hold values from -12 to 12
Outputs:
- layer_out: bfloat16 [4096, 2048], P(('dp', 'expert'))
- tokens_grad: bfloat16 [4096, 2048], P(('dp', 'expert'))
- gate_grad: bfloat16 [4096, 4], P(('dp', 'expert'))
- w_in_new: bfloat16 [8, 2048, 1536], P('expert', 'dp')
- w_out_new: bfloat16 [8, 768, 2048], P('expert', 'dp')
- mom_in_new: float32 [8, 2048, 1536], P('expert', 'dp')
- mom_out_new: float32 [8, 768, 2048], P('expert', 'dp')
Inputs may be any that keep to these rules, and one draw needn't show every extreme that they name: `expert_ids`: each row names 4 different experts. Among the 128 tokens of one device (aligned blocks of rows), no expert is named more than 96 times, a bound that some block reaches.
All inputs are finite; a program needn't handle non-finite values.
Results may differ from a plain program's by a relative error of at most 0.009.
Values may be sent and summed in bfloat16 or wider, within the bound.
A program may use at most 128 MiB of HBM per device.

v0:
```python
import jax
import jax.numpy as jnp
from jax import lax
from jax.sharding import PartitionSpec as P

FF = 768


beta_one = 0.9
beta_two = 0.99
learn_rate = 0.02
decay_rate = 0.1


def to_experts(buffer, groups, local_count, capacity):
    trailing = buffer.shape[2:]
    shaped = buffer.reshape((groups, local_count, capacity) + trailing)
    return jnp.swapaxes(shaped, 0, 1).reshape((local_count, groups * capacity) + trailing)


def from_experts(buffer, groups, local_count, capacity):
    trailing = buffer.shape[2:]
    shaped = buffer.reshape((local_count, groups, capacity) + trailing)
    return jnp.swapaxes(shaped, 0, 1).reshape((groups, local_count * capacity) + trailing)


def forward_pass(expert_in, expert_gates, full_in, full_out):
    pre = jnp.einsum("erd,edf->erf", expert_in, full_in, preferred_element_type=jnp.float32)
    gate_part = pre[..., :FF]
    up_part = pre[..., FF:]
    sig_part = jax.nn.sigmoid(gate_part)
    activated = gate_part * sig_part
    hidden = (activated * up_part).astype(jnp.bfloat16)
    expert_out = jnp.einsum("erf,efd->erd", hidden, full_out, preferred_element_type=jnp.float32)
    gate_col = expert_gates.astype(jnp.float32)[..., None]
    weighted = (gate_col * expert_out).astype(jnp.bfloat16)
    return (up_part, gate_part, sig_part, activated, hidden, expert_out, weighted)


def lion_update(weight, moment, grad):
    blend = beta_one * moment + (1.0 - beta_one) * grad
    direction = blend / jnp.sqrt(blend * blend + 1.0)
    wide = weight.astype(jnp.float32)
    new_weight = (wide - learn_rate * (direction + decay_rate * wide)).astype(jnp.bfloat16)
    new_moment = beta_two * moment + (1.0 - beta_two) * grad
    return (new_weight, new_moment)


def body(tokens, cotangent, expert_ids, gate_probs, w_in, w_out, mom_in, mom_out):
    groups = lax.axis_size("expert")
    local_count = w_in.shape[0]
    experts = groups * local_count
    tok_rows, top_count = expert_ids.shape
    model_width = tokens.shape[1]
    capacity = 3 * tok_rows * top_count // (2 * experts)
    slot_total = experts * capacity
    flat_ids = expert_ids.reshape(-1)
    onehot = (flat_ids[:, None] == jnp.arange(experts, dtype=jnp.int32)[None, :]).astype(jnp.int32)
    position = jnp.sum((jnp.cumsum(onehot, axis=0) - onehot) * onehot, axis=1)
    slot_ids = flat_ids * capacity + position
    matches = (slot_ids[:, None] == jnp.arange(slot_total, dtype=jnp.int32)[None, :]).reshape(
        tok_rows, top_count, slot_total
    )
    placement = jnp.sum(matches.astype(jnp.int32), axis=1).astype(jnp.bfloat16)
    match_float = matches.astype(jnp.float32)
    gate_slots = jnp.einsum("tk,tks->s", gate_probs.astype(jnp.float32), match_float).astype(
        jnp.bfloat16
    )
    gate_slots = gate_slots.reshape(groups, local_count * capacity)
    x_slots = jnp.einsum("ts,td->sd", placement, tokens, preferred_element_type=jnp.float32).astype(
        jnp.bfloat16
    )
    x_slots = x_slots.reshape(groups, local_count * capacity, model_width)
    cot_slots = jnp.einsum(
        "ts,td->sd", placement, cotangent, preferred_element_type=jnp.float32
    ).astype(jnp.bfloat16)
    cot_slots = cot_slots.reshape(groups, local_count * capacity, model_width)
    full_in, full_out = (
        lax.all_gather(w_in, "dp", axis=1, tiled=True),
        lax.all_gather(w_out, "dp", axis=1, tiled=True),
    )
    recv_x, recv_gate, recv_cot = (
        lax.all_to_all(x_slots, "expert", split_axis=0, concat_axis=0, tiled=True),
        lax.all_to_all(gate_slots, "expert", split_axis=0, concat_axis=0, tiled=True),
        lax.all_to_all(cot_slots, "expert", split_axis=0, concat_axis=0, tiled=True),
    )
    expert_in = to_experts(recv_x, groups, local_count, capacity)
    expert_gates = to_experts(recv_gate, groups, local_count, capacity)
    up_part, gate_part, sig_part, activated, hidden, expert_out, weighted = forward_pass(
        expert_in, expert_gates, full_in, full_out
    )
    expert_cot = to_experts(recv_cot, groups, local_count, capacity)
    slot_gate = jnp.sum(expert_cot.astype(jnp.float32) * expert_out, axis=-1).astype(jnp.bfloat16)
    out_grad = (
        expert_gates.astype(jnp.float32)[..., None] * expert_cot.astype(jnp.float32)
    ).astype(jnp.bfloat16)
    hidden_grad = jnp.einsum("erd,efd->erf", out_grad, full_out, preferred_element_type=jnp.float32)
    slope = sig_part * (1.0 + gate_part * (1.0 - sig_part))
    pre_grad = jnp.concatenate(
        [hidden_grad * up_part * slope, hidden_grad * activated], axis=-1
    ).astype(jnp.bfloat16)
    slot_grad = jnp.einsum(
        "erf,edf->erd", pre_grad, full_in, preferred_element_type=jnp.float32
    ).astype(jnp.bfloat16)
    returned = (
        lax.all_to_all(
            from_experts(weighted, groups, local_count, capacity),
            "expert",
            split_axis=0,
            concat_axis=0,
            tiled=True,
        ),
        lax.all_to_all(
            from_experts(slot_grad, groups, local_count, capacity),
            "expert",
            split_axis=0,
            concat_axis=0,
            tiled=True,
        ),
        lax.all_to_all(
            from_experts(slot_gate, groups, local_count, capacity),
            "expert",
            split_axis=0,
            concat_axis=0,
            tiled=True,
        ),
    )
    layer_slots = returned[0].reshape(slot_total, model_width)
    grad_slots = returned[1].reshape(slot_total, model_width)
    gate_back = returned[2].reshape(slot_total).astype(jnp.float32)
    layer_out = jnp.einsum(
        "ts,sd->td", placement, layer_slots, preferred_element_type=jnp.float32
    ).astype(jnp.bfloat16)
    tokens_grad = jnp.einsum(
        "ts,sd->td", placement, grad_slots, preferred_element_type=jnp.float32
    ).astype(jnp.bfloat16)
    gate_grad = jnp.einsum("tks,s->tk", match_float, gate_back).astype(jnp.bfloat16)
    term_in = jnp.einsum("erd,erf->edf", expert_in, pre_grad, preferred_element_type=jnp.float32)
    term_out = jnp.einsum("erf,erd->efd", hidden, out_grad, preferred_element_type=jnp.float32)
    grad_in, grad_out = (
        lax.psum_scatter(
            term_in.astype(jnp.bfloat16), "dp", scatter_dimension=1, tiled=True
        ).astype(jnp.float32),
        lax.psum_scatter(
            term_out.astype(jnp.bfloat16), "dp", scatter_dimension=1, tiled=True
        ).astype(jnp.float32),
    )
    w_in_new, mom_in_new = lion_update(w_in, mom_in, grad_in)
    w_out_new, mom_out_new = lion_update(w_out, mom_out, grad_out)
    return (layer_out, tokens_grad, gate_grad, w_in_new, w_out_new, mom_in_new, mom_out_new)


def solution(mesh):
    in_specs = (
        P(("dp", "expert"), None),
        P(("dp", "expert"), None),
        P(("dp", "expert"), None),
        P(("dp", "expert"), None),
        P("expert", "dp", None),
        P("expert", "dp", None),
        P("expert", "dp", None),
        P("expert", "dp", None),
    )
    out_specs = (
        P(("dp", "expert"), None),
        P(("dp", "expert"), None),
        P(("dp", "expert"), None),
        P("expert", "dp", None),
        P("expert", "dp", None),
        P("expert", "dp", None),
        P("expert", "dp", None),
    )
    return jax.shard_map(body, mesh=mesh, in_specs=in_specs, out_specs=out_specs, check_vma=False)
```

profile of v0, /device:TPU:0, one launch (start us, length us, event | category | flops | bytes accessed | tf_op | source)
XLA Modules:
  0.0 384.0 jit_solution(16317268752240340892)
XLA Ops:
  7.2 0.7 all-gather.3.cloned.1.call-update
  7.9 0.8 copy.41
  8.9 1.1 reduce-window.6
  10.6 0.7 multiply_add_fusion
  11.3 1.1 fusion.39
  12.4 0.7 all_to_all.29
  13.1 6.3 %all-to-all-start = ((bf16[8,1,96]{2,1,0:T(2,128)(2,1)}), bf16[8,1,96]{2,1,0:T(2,128)(2,1)S(1)}, u32[]{:S(2)}, u32[]{:S(2)}) async-start(bf16[8,1,96]{2,1,0:T(2,128)(2,1)} %all_to_all.29), calls=%async_computation | async-start | bytes 8192 | tf_op jit(solution)/shard_map/all_to_all | solution.py:84
  19.7 2.7 convolution_convert_fusion.3
  22.4 2.5 all-to-all-done
  24.9 4.6 %all-to-all-start.1 = ((bf16[8,96,2048]{2,1,0:T(8,128)(2,1)}), bf16[8,96,2048]{2,1,0:T(8,128)(2,1)}, u32[]{:S(2)}, u32[]{:S(2)}) async-start(bf16[8,96,2048]{2,1,0:T(8,128)(2,1)} %bitcast.91), calls=%async_computation.1 | async-start | bytes 6291456 | tf_op jit(solution)/shard_map/all_to_all | solution.py:83
  29.5 2.7 convolution_convert_fusion.2
  32.2 68.9 %all-to-all-done.1 = bf16[8,96,2048]{2,1,0:T(8,128)(2,1)} async-done(((bf16[8,96,2048]{2,1,0:T(8,128)(2,1)}), bf16[8,96,2048]{2,1,0:T(8,128)(2,1)}, u32[]{:S(2)}, u32[]{:S(2)}) %all-to-all-start.1) | async-done | bytes 3145760 | tf_op jit(solution)/shard_map/all_to_all | solution.py:83
  101.1 3.7 all-to-all-start.3
  104.8 0.7 all-gather.5.cloned.1.call-update
  105.6 9.6 %fusion.6 = f32[1,768,1536]{2,1,0:T(8,128)} fusion(bf16[768,2048]{1,0:T(8,128)(2,1)} %bitcast.4, bf16[1,2048,1536]{2,1,0:T(8,128)(2,1)} %all-gather.3.cloned.1.call-done), kind=kOutput, calls=%fused_computation.14 | convolution fusion | flops 4831838208 | bytes 14155776 | tf_op jit(solution)/shard_map/erd,edf->erf/dot_general | solution.py:28
  115.2 37.6 %all-gather.5.cloned.1.call-done = bf16[1,768,2048]{2,1,0:T(8,128)(2,1)} async-done(((bf16[1,192,2048]{2,1,0:T(8,128)(2,1)}), bf16[1,768,2048]{2,1,0:T(8,128)(2,1)}) %all-gather.5.cloned.1.call-update) | async-done | bytes 3145744 | tf_op jit(solution)/shard_map/all_gather | solution.py:80
  152.8 23.4 %all-to-all-done.3 = bf16[8,96,2048]{2,1,0:T(8,128)(2,1)S(1)} async-done(((bf16[8,96,2048]{2,1,0:T(8,128)(2,1)}), bf16[8,96,2048]{2,1,0:T(8,128)(2,1)S(1)}, u32[]{:S(2)}, u32[]{:S(2)}) %all-to-all-start.3) | async-done | bytes 3145760 | tf_op jit(solution)/shard_map/all_to_all | solution.py:85
  176.2 7.3 %fusion.38 = (bf16[768,768]{1,0:T(8,128)(2,1)}, bf16[768,768]{1,0:T(8,128)(2,1)}, bf16[768,768]{1,0:T(8,128)(2,1)S(1)}) fusion(f32[1,768,1536]{2,1,0:T(8,128)} %fusion.6, bf16[1,768,2048]{2,1,0:T(8,128)(2,1)} %all-gather.5.cloned.1.call-done, f32[768]{0:T(1024)S(1)} %reshape.241, bf16[1,768,1,1,1,1,2048]{6,1,5,4,3,2,0:T(8,128)(2,1)S(1)} %bitcast.92), kind=kOutput, calls=%fused_computation.58 | convolution fusion | flops 2429485056 | bytes 14552064 | tf_op jit(solution)/shard_map/erd,efd->erf/dot_general | solution.py:97
  183.4 1.0 copy-done.5
  184.5 4.2 %fusion.22 = bf16[1,768,2048]{2,1,0:T(8,128)(2,1)} fusion(bf16[768,768]{1,0:T(8,128)(2,1)S(1)} %get-tuple-element.13, f32[768]{0:T(1024)S(1)} %reshape.241, bf16[1,768,1,1,1,1,2048]{6,1,5,4,3,2,0:T(8,128)(2,1)S(1)} %bitcast.93), kind=kOutput, calls=%fused_computation.29 | convolution fusion | flops 2422210560 | bytes 7474176 | tf_op jit(solution)/shard_map/erf,erd->efd/dot_general | solution.py:139
  189.0 9.1 %fusion = bf16[1,2048,1536]{2,1,0:T(8,128)(2,1)} fusion(bf16[768,2048]{1,0:T(8,128)(2,1)} %bitcast.4, bf16[768,768]{1,0:T(8,128)(2,1)} %get-tuple-element.8, bf16[768,768]{1,0:T(8,128)(2,1)} %get-tuple-element.7), kind=kOutput, calls=%fused_computation.1 | convolution fusion | flops 4839702528 | bytes 11796480 | tf_op jit(solution)/shard_map/erd,erf->edf/dot_general | solution.py:138
  198.1 6.8 %fusion.1 = (bf16[768]{0:T(1024)(128)(2,1)S(1)}, bf16[768,2048]{1,0:T(8,128)(2,1)}) fusion(bf16[8,96,2048]{2,1,0:T(8,128)(2,1)S(1)} %all-to-all-done.3, f32[768]{0:T(1024)S(1)} %reshape.241, bf16[768,768]{1,0:T(8,128)(2,1)} %copy-done.5, bf16[1,768,2048]{2,1,0:T(8,128)(2,1)} %all-gather.5.cloned.1.call-done), kind=kOutput, calls=%fused_computation.3 | convolution fusion | flops 2423782656 | bytes 10621440 | tf_op jit(solution)/shard_map/erf,efd->erd/dot_general | solution.py:34
  204.9 7.9 %all_to_all.36 = bf16[8,1,96]{2,1,0:T(2,128)(2,1)S(1)} all-to-all(bf16[8,1,96]{2,1,0:T(2,128)(2,1)S(1)} %convert_element_type.204), channel_id=1, replica_groups=mesh['dp'=4,'expert'=8] {'expert'}, dimensions={0} | all-to-all | bytes 3072 | tf_op jit(solution)/shard_map/all_to_all | solution.py:120
  212.8 3.7 all-to-all-start.2
  216.5 9.1 %fusion.9 = bf16[768,2048]{1,0:T(8,128)(2,1)} fusion(bf16[1,2048,1536]{2,1,0:T(8,128)(2,1)} %all-gather.3.cloned.1.call-done, bf16[768,768]{1,0:T(8,128)(2,1)} %get-tuple-element.8, bf16[768,768]{1,0:T(8,128)(2,1)} %get-tuple-element.7), kind=kOutput, calls=%fused_computation.18 | convolution fusion | flops 4838129664 | bytes 11796480 | tf_op jit(solution)/shard_map/erf,edf->erd/dot_general | solution.py:102
  225.6 62.4 %all-to-all-done.2 = bf16[8,96,2048]{2,1,0:T(8,128)(2,1)S(1)} async-done(((bf16[8,96,2048]{2,1,0:T(8,128)(2,1)}), bf16[8,96,2048]{2,1,0:T(8,128)(2,1)S(1)}, u32[]{:S(2)}, u32[]{:S(2)}) %all-to-all-start.2) | async-done | bytes 3145760 | tf_op jit(solution)/shard_map/all_to_all | solution.py:106
  287.9 4.4 %all-to-all-start.4 = ((bf16[8,96,2048]{2,1,0:T(8,128)(2,1)}), bf16[8,96,2048]{2,1,0:T(8,128)(2,1)}, u32[]{:S(2)}, u32[]{:S(2)}) async-start(bf16[8,96,2048]{2,1,0:T(8,128)(2,1)} %bitcast.94), calls=%async_computation.4 | async-start | bytes 6291456 | tf_op jit(solution)/shard_map/all_to_all | solution.py:113
  293.5 1.4 convolution_convert_fusion.5
  294.9 69.0 %all-to-all-done.4 = bf16[8,96,2048]{2,1,0:T(8,128)(2,1)} async-done(((bf16[8,96,2048]{2,1,0:T(8,128)(2,1)}), bf16[8,96,2048]{2,1,0:T(8,128)(2,1)}, u32[]{:S(2)}, u32[]{:S(2)}) %all-to-all-start.4) | async-done | bytes 3145760 | tf_op jit(solution)/shard_map/all_to_all | solution.py:113
  363.9 3.3 convolution_convert_fusion.4
  367.2 4.0 %fusion.31 = (f32[1,192,2048]{2,1,0:T(8,128)}, bf16[1,192,2048]{2,1,0:T(8,128)(2,1)}) fusion(bf16[1,192,2048]{2,1,0:T(8,128)(2,1)} %reduce-scatter.5.cloned.1.call-done, f32[1,192,2048]{2,1,0:T(8,128)} %param.15, bf16[1,192,2048]{2,1,0:T(8,128)(2,1)S(1)} %copy-done.3), kind=kLoop, calls=%fused_computation.49 | loop fusion | flops 6291456 | bytes 5505024 | tf_op jit(solution)/shard_map/add | solution.py:45
  371.2 6.2 %fusion.16 = (f32[1,512,1536]{2,1,0:T(8,128)}, bf16[1,512,1536]{2,1,0:T(8,128)(2,1)}) fusion(bf16[1,512,1536]{2,1,0:T(8,128)(2,1)} %reduce-scatter.3.cloned.1.call-done, f32[1,512,1536]{2,1,0:T(8,128)} %param.14, bf16[1,512,1536]{2,1,0:T(8,128)(2,1)S(1)} %copy-done.2), kind=kLoop, calls=%fused_computation.23 | loop fusion | flops 12582912 | bytes 11010048 | tf_op jit(solution)/shard_map/add | solution.py:45
  (38 shorter events, 2.7 us)
Async XLA Ops:
  7.2 12.6 %copy-start = (bf16[128,2048]{1,0:T(8,128)(2,1)S(1)}, bf16[128,2048]{1,0:T(8,128)(2,1)}, u32[]{:S(2)}) copy-start(bf16[128,2048]{1,0:T(8,128)(2,1)} %param.8) | copy-start | bytes 1572868
  7.2 98.4 %all-gather.3.cloned.1.call-start = ((), (), s32[]{:S(2)}) async-start(), calls=%async_computation.8 | async-start | bytes 7864320 | tf_op jit(solution)/shard_map/all_gather | solution.py:79
  13.1 11.8 %all-to-all-start = ((bf16[8,1,96]{2,1,0:T(2,128)(2,1)}), bf16[8,1,96]{2,1,0:T(2,128)(2,1)S(1)}, u32[]{:S(2)}, u32[]{:S(2)}) async-start(bf16[8,1,96]{2,1,0:T(2,128)(2,1)} %all_to_all.29), calls=%async_computation | async-start | bytes 8192 | tf_op jit(solution)/shard_map/all_to_all | solution.py:84
  24.9 4.6 %copy-start.4 = (bf16[128,2048]{1,0:T(8,128)(2,1)S(1)}, bf16[128,2048]{1,0:T(8,128)(2,1)}, u32[]{:S(2)}) copy-start(bf16[128,2048]{1,0:T(8,128)(2,1)} %param.9) | copy-start | bytes 1572868
  24.9 76.1 %all-to-all-start.1 = ((bf16[8,96,2048]{2,1,0:T(8,128)(2,1)}), bf16[8,96,2048]{2,1,0:T(8,128)(2,1)}, u32[]{:S(2)}, u32[]{:S(2)}) async-start(bf16[8,96,2048]{2,1,0:T(8,128)(2,1)} %bitcast.91), calls=%async_computation.1 | async-start | bytes 6291456 | tf_op jit(solution)/shard_map/all_to_all | solution.py:83
  101.1 75.1 %all-to-all-start.3 = ((bf16[8,96,2048]{2,1,0:T(8,128)(2,1)}), bf16[8,96,2048]{2,1,0:T(8,128)(2,1)S(1)}, u32[]{:S(2)}, u32[]{:S(2)}) async-start(bf16[8,96,2048]{2,1,0:T(8,128)(2,1)} %bitcast.11), calls=%async_computation.3 | async-start | bytes 6291456 | tf_op jit(solution)/shard_map/all_to_all | solution.py:85
  104.7 48.1 %all-gather.5.cloned.1.call-start = ((), (), s32[]{:S(2)}) async-start(), calls=%async_computation.9 | async-start | bytes 3932160 | tf_op jit(solution)/shard_map/all_gather | solution.py:80
  105.5 261.7 %reduce-scatter.5.cloned.1.call-start = ((), (), s32[]{:S(2)}) async-start(), calls=%async_computation.11 | async-start | bytes 3932160 | tf_op jit(solution)/shard_map/reduce_scatter | solution.py:144
  183.4 1.0 copy-start.5
  188.7 182.5 %reduce-scatter.3.cloned.1.call-start = ((), (), s32[]{:S(2)}) async-start(), calls=%async_computation.10 | async-start | bytes 7864320 | tf_op jit(solution)/shard_map/reduce_scatter | solution.py:141
  212.8 75.1 %all-to-all-start.2 = ((bf16[8,96,2048]{2,1,0:T(8,128)(2,1)}), bf16[8,96,2048]{2,1,0:T(8,128)(2,1)S(1)}, u32[]{:S(2)}, u32[]{:S(2)}) async-start(bf16[8,96,2048]{2,1,0:T(8,128)(2,1)} %bitcast.95), calls=%async_computation.2 | async-start | bytes 6291456 | tf_op jit(solution)/shard_map/all_to_all | solution.py:106
  287.9 76.0 %all-to-all-start.4 = ((bf16[8,96,2048]{2,1,0:T(8,128)(2,1)}), bf16[8,96,2048]{2,1,0:T(8,128)(2,1)}, u32[]{:S(2)}, u32[]{:S(2)}) async-start(bf16[8,96,2048]{2,1,0:T(8,128)(2,1)} %bitcast.94), calls=%async_computation.4 | async-start | bytes 6291456 | tf_op jit(solution)/shard_map/all_to_all | solution.py:113
  294.9 72.3 %copy-start.3 = (bf16[1,192,2048]{2,1,0:T(8,128)(2,1)S(1)}, bf16[1,192,2048]{2,1,0:T(8,128)(2,1)}, u32[]{:S(2)}) copy-start(bf16[1,192,2048]{2,1,0:T(8,128)(2,1)} %param.13) | copy-start | bytes 2359300
  367.2 4.0 %copy-start.2 = (bf16[1,512,1536]{2,1,0:T(8,128)(2,1)S(1)}, bf16[1,512,1536]{2,1,0:T(8,128)(2,1)}, u32[]{:S(2)}) copy-start(bf16[1,512,1536]{2,1,0:T(8,128)(2,1)} %param.12) | copy-start | bytes 4718596
  367.2 10.3 %copy-start.1 = (bf16[128,2048]{1,0:T(8,128)(2,1)S(1)}, bf16[128,2048]{1,0:T(8,128)(2,1)}, u32[]{:S(2)}) copy-start(bf16[128,2048]{1,0:T(8,128)(2,1)} %param.8) | copy-start | bytes 1572868
Sparse Core Ops, SparseCore 0:
  9.9 72.8 all-gather.2
  107.4 45.3 all-gather.4
  188.9 42.8 reduce-scatter.4
  234.5 70.1 reduce-scatter.2
where the time goes:
time: 385 us; the launch traced here: 384 us
  waiting for transfers between devices  265 us (69%)
  matrix products  57.6 us (15%)
  starting transfers between devices  23 us (6%)
  between operations  13.9 us (4%)
  other arithmetic  13.1 us (3%)
  blocking collectives  7.91 us (2%)
    all_to_all x1, waiting for transfers between devices, body(): lax.all_to_all(from_experts(slot_grad, groups, local_count, capacity), 'e...  69 us
    all_to_all x1, waiting for transfers between devices, body(): lax.all_to_all(x_slots, 'expert', split_axis=0, concat_axis=0, tiled=True)  68.9 us
    all_to_all x1, waiting for transfers between devices, body(): lax.all_to_all(from_experts(weighted, groups, local_count, capacity), 'ex...  62.4 us
    all_gather x1, waiting for transfers between devices, body(): lax.all_gather(w_out, 'dp', axis=1, tiled=True)  37.6 us
    all_to_all x1, waiting for transfers between devices, body(): lax.all_to_all(cot_slots, 'expert', split_axis=0, concat_axis=0, tiled=True)  23.4 us
    add x2, other arithmetic, lion_update(): new_moment = beta_two * moment + (1.0 - beta_two) * grad  10.3 us
    dot_general x1, matrix products, forward_pass(): jnp.einsum('erd,edf->erf', expert_in, full_in, preferred_element_type=jnp...  9.6 us
    dot_general x1, matrix products, body(): jnp.einsum('erf,edf->erd', pre_grad, full_in, preferred_element_type=jnp....  9.08 us
  transfers between devices with their start and end apart: 9, of which 6 were waited for; matrix products, arithmetic and copies ran while one was open for 14% of the time, Pallas kernels for 0%

commit v1 on v0

v1 whole, which is shorter than its diff:
```python
import jax
import jax.numpy as jnp
from jax import lax
from jax.sharding import PartitionSpec as P

FF = 768


beta_one = 0.9
beta_two = 0.99
learn_rate = 0.02
decay_rate = 0.1


def lion_update(weight, moment, grad):
    blend = beta_one * moment + (1.0 - beta_one) * grad
    direction = blend / jnp.sqrt(blend * blend + 1.0)
    wide = weight.astype(jnp.float32)
    new_weight = (wide - learn_rate * (direction + decay_rate * wide)).astype(jnp.bfloat16)
    new_moment = beta_two * moment + (1.0 - beta_two) * grad
    return (new_weight, new_moment)


def dot(a, b, contract):
    return lax.dot_general(a, b, (contract, ((), ())), preferred_element_type=jnp.float32)


def body(tokens, cotangent, expert_ids, gate_probs, w_in, w_out, mom_in, mom_out):
    groups = lax.axis_size("expert")
    me = lax.axis_index("expert")
    tok_rows = tokens.shape[0]
    rows = lax.all_gather(tokens, "expert", axis=0, tiled=True)
    cots = lax.all_gather(cotangent, "expert", axis=0, tiled=True)
    hits = (expert_ids[:, :, None] == jnp.arange(groups, dtype=jnp.int32)[None, None, :])
    gates = jnp.sum(jnp.where(hits, gate_probs.astype(jnp.float32)[:, :, None], 0.0), axis=1)
    gates = lax.all_to_all(
        gates.astype(jnp.bfloat16).T.reshape(groups, tok_rows), "expert", 0, 0, tiled=True
    )
    gate_col = gates.reshape(-1).astype(jnp.float32)[:, None]
    full_in = lax.all_gather(w_in[0], "dp", axis=0, tiled=True)
    full_out = lax.all_gather(w_out[0], "dp", axis=0, tiled=True)

    pre = dot(rows, full_in, ((1,), (0,)))
    gate_part = pre[:, :FF]
    up_part = pre[:, FF:]
    sig_part = jax.nn.sigmoid(gate_part)
    activated = gate_part * sig_part
    hidden = (activated * up_part).astype(jnp.bfloat16)
    out_grad = (gate_col * cots.astype(jnp.float32)).astype(jnp.bfloat16)
    term_out = dot(hidden, out_grad, ((0,), (0,))).astype(jnp.bfloat16)
    grad_out = lax.psum_scatter(term_out, "dp", scatter_dimension=0, tiled=True)
    expert_out = dot(hidden, full_out, ((1,), (0,)))
    weighted = (gate_col * expert_out).astype(jnp.bfloat16)
    slot_gate = jnp.sum(cots.astype(jnp.float32) * expert_out, axis=-1).astype(jnp.bfloat16)
    layer_out = lax.psum_scatter(weighted, "expert", scatter_dimension=0, tiled=True)
    gate_back = lax.all_to_all(slot_gate.reshape(groups, tok_rows), "expert", 0, 0, tiled=True)
    hidden_grad = dot(out_grad, full_out, ((1,), (1,)))
    slope = sig_part * (1.0 + gate_part * (1.0 - sig_part))
    pre_grad = jnp.concatenate(
        [hidden_grad * up_part * slope, hidden_grad * activated], axis=-1
    ).astype(jnp.bfloat16)
    term_in = dot(rows, pre_grad, ((0,), (0,))).astype(jnp.bfloat16)
    grad_in = lax.psum_scatter(term_in, "dp", scatter_dimension=0, tiled=True)
    slot_grad = dot(pre_grad, full_in, ((1,), (1,))).astype(jnp.bfloat16)
    tokens_grad = lax.psum_scatter(slot_grad, "expert", scatter_dimension=0, tiled=True)
    gate_grad = jnp.sum(
        jnp.where(hits, gate_back.astype(jnp.float32).T[:, None, :], 0.0), axis=2
    ).astype(jnp.bfloat16)
    w_in_new, mom_in_new = lion_update(w_in, mom_in, grad_in.astype(jnp.float32)[None])
    w_out_new, mom_out_new = lion_update(w_out, mom_out, grad_out.astype(jnp.float32)[None])
    return (layer_out, tokens_grad, gate_grad, w_in_new, w_out_new, mom_in_new, mom_out_new)


def solution(mesh):
    rows_spec = P(("dp", "expert"), None)
    weight_spec = P("expert", "dp", None)
    in_specs = (rows_spec,) * 4 + (weight_spec,) * 4
    out_specs = (rows_spec,) * 3 + (weight_spec,) * 4
    return jax.shard_map(body, mesh=mesh, in_specs=in_specs, out_specs=out_specs, check_vma=False)
```

time: 385 us -> 485 us (1.26)
  waiting for transfers between devices: 265 us -> 372 us
  starting transfers between devices: 23 us -> 4.03 us
  local copies, waits for them, and re-layouts: 3.39 us -> 13.8 us
    all_to_all x5 -> x1, waiting for transfers between devices: 226 us -> 5.34 us  [body(): lax.all_to_all(slot_gate.reshape(groups, tok_rows), 'expert', 0, 0, tiled...]
    all_gather x2 -> x4, waiting for transfers between devices: 37.6 us -> 201 us  [the longest x1 70.8 us: body(): full_in = lax.all_gather(w_in[0], 'dp', axis=0, tiled=True)]
    reduce_scatter x2 -> x4, waiting for transfers between devices: 0.01 us -> 163 us  [the longest x1 69 us: body(): grad_in = lax.psum_scatter(term_in, 'dp', scatter_dimension=0, tiled=True)]
    all_to_all x5 -> x1, starting transfers between devices: 22.7 us -> 3.31 us  [body(): lax.all_to_all(slot_gate.reshape(groups, tok_rows), 'expert', 0, 0, tiled...]
    unnamed x13 -> x16, local copies, waits for them, and re-layouts: 1.86 us -> 13.2 us
    convert_element_type x4, other arithmetic: 0.62 us -> 6.84 us  [the longest x1 5.95 us: body(): weighted = (gate_col * expert_out).astype(jnp.bfloat16)]
    dot_general x12 -> x6, matrix products: 57.6 us -> 55.1 us  [dot(): lax.dot_general(a, b, (contract, ((), ())), preferred_element_type=jnp.fl...]
  transfers between devices with their start and end apart: 9 -> 9, of which waited for: 6 -> 9; matrix products, arithmetic and copies ran while one was open for 14% -> 14% of each run, Pallas kernels for 0% -> 0%
where the time goes in v1:
time: 485 us; the launch traced here: 484 us
  waiting for transfers between devices  372 us (77%)
  matrix products  55.1 us (11%)
  other arithmetic  17.3 us (4%)
  between operations  14.2 us (3%)
  local copies, waits for them, and re-layouts  13.8 us (3%)
  blocking collectives  7.91 us (2%)
    all_gather x1, waiting for transfers between devices, body(): full_in = lax.all_gather(w_in[0], 'dp', axis=0, tiled=True)  70.8 us
    reduce_scatter x1, waiting for transfers between devices, body(): grad_in = lax.psum_scatter(term_in, 'dp', scatter_dimension=0, tiled=True)  69 us
    dot_general x6, matrix products, dot(): lax.dot_general(a, b, (contract, ((), ())), preferred_element_type=jnp.fl...  55.1 us
    reduce_scatter x1, waiting for transfers between devices, body(): lax.psum_scatter(weighted, 'expert', scatter_dimension=0, tiled=True)  51 us
    all_gather x1, waiting for transfers between devices, body(): rows = lax.all_gather(tokens, 'expert', axis=0, tiled=True)  49.5 us
    all_gather x1, waiting for transfers between devices, body(): cots = lax.all_gather(cotangent, 'expert', axis=0, tiled=True)  48.6 us
    reduce_scatter x1, waiting for transfers between devices, body(): lax.psum_scatter(slot_grad, 'expert', scatter_dimension=0, tiled=True)  41.9 us
    all_gather x1, waiting for transfers between devices, body(): full_out = lax.all_gather(w_out[0], 'dp', axis=0, tiled=True)  32.4 us
  transfers between devices with their start and end apart: 9, of which 9 were waited for; matrix products, arithmetic and copies ran while one was open for 14% of the time, Pallas kernels for 0%

profile of v1, /device:TPU:0, one launch (start us, length us, event | category | flops | bytes accessed | tf_op | source)
XLA Modules:
  0.0 484.3 jit_solution(4084922147626303723)
XLA Ops:
  7.2 0.7 all-gather.7.cloned.1.call-update
  7.9 0.7 all-gather.11.cloned.1.call-update
  8.7 0.7 all-gather.13.cloned.1.call-update
  10.0 49.5 %all-gather.7.cloned.1.call-done = bf16[1024,2048]{1,0:T(8,128)(2,1)} async-done(((bf16[128,2048]{1,0:T(8,128)(2,1)}), bf16[1024,2048]{1,0:T(8,128)(2,1)}) %all-gather.7.cloned.1.call-update) | async-done | bytes 4194320 | tf_op jit(solution)/shard_map/all_gather | solution.py:32
  59.5 70.8 %all-gather.11.cloned.1.call-done = bf16[1,2048,1536]{2,1,0:T(8,128)(2,1)} async-done(((bf16[1,512,1536]{2,1,0:T(8,128)(2,1)}), bf16[1,2048,1536]{2,1,0:T(8,128)(2,1)}) %all-gather.11.cloned.1.call-update) | async-done | bytes 6291472 | tf_op jit(solution)/shard_map/all_gather | solution.py:40
  130.2 10.0 %fusion.5 = f32[1024,1536]{1,0:T(8,128)S(1)} fusion(bf16[1024,2048]{1,0:T(8,128)(2,1)} %all-gather.7.cloned.1.call-done, bf16[1,2048,1536]{2,1,0:T(8,128)(2,1)} %all-gather.11.cloned.1.call-done), kind=kOutput, calls=%fused_computation.9 | convolution fusion | flops 6442450944 | bytes 16777216 | tf_op jit(solution)/shard_map/dot_general | solution.py:25
  140.2 2.6 copy-done.1
  142.8 0.9 multiply_convert_fusion.3
  143.7 32.4 %all-gather.13.cloned.1.call-done = bf16[1,768,2048]{2,1,0:T(8,128)(2,1)} async-done(((bf16[1,192,2048]{2,1,0:T(8,128)(2,1)}), bf16[1,768,2048]{2,1,0:T(8,128)(2,1)}) %all-gather.13.cloned.1.call-update) | async-done | bytes 3145744 | tf_op jit(solution)/shard_map/all_gather | solution.py:41
  176.1 48.6 %all-gather.9.cloned.1.call-done = bf16[1024,2048]{1,0:T(8,128)(2,1)} async-done(((bf16[128,2048]{1,0:T(8,128)(2,1)}), bf16[1024,2048]{1,0:T(8,128)(2,1)}) %all-gather.9.cloned.1.call-update) | async-done | bytes 4194320 | tf_op jit(solution)/shard_map/all_gather | solution.py:33
  224.7 8.2 %fusion.1 = (bf16[1024]{0:T(1024)(128)(2,1)S(1)}, f32[1024,2048]{1,0:T(8,128)}) fusion(bf16[1024,2048]{1,0:T(8,128)(2,1)} %all-gather.9.cloned.1.call-done, bf16[1024,768]{1,0:T(8,128)(2,1)S(1)} %multiply_convert_fusion.3, bf16[1,768,2048]{2,1,0:T(8,128)(2,1)} %all-gather.13.cloned.1.call-done), kind=kOutput, calls=%fused_computation.3 | convolution fusion | flops 3227515904 | bytes 17303552 | tf_op jit(solution)/shard_map/dot_general | solution.py:25
  232.9 0.6 copy.63
  233.5 3.3 all-to-all-start.1
  236.9 5.3 %all-to-all-done.1 = bf16[8,1,128]{2,1,0:T(2,128)(2,1)S(1)} async-done(((bf16[8,1,128]{2,1,0:T(2,128)(2,1)}), bf16[8,1,128]{2,1,0:T(2,128)(2,1)S(1)}, u32[]{:S(2)}, u32[]{:S(2)}) %all-to-all-start.1) | async-done | bytes 2080 | tf_op jit(solution)/shard_map/all_to_all | solution.py:56
  242.3 0.6 select_reduce_fusion
  242.9 7.9 %all_to_all.15 = bf16[8,1,128]{2,1,0:T(2,128)(2,1)S(1)} all-to-all(bf16[8,1,128]{2,1,0:T(2,128)(2,1)S(1)} %copy.59), channel_id=1, replica_groups=mesh['dp'=4,'expert'=8] {'expert'}, dimensions={0} | all-to-all | bytes 4096 | tf_op jit(solution)/shard_map/all_to_all | solution.py:36
  250.8 7.3 %convolution_convert_fusion.1 = bf16[768,2048]{1,0:T(8,128)(2,1)} fusion(bf16[1024,768]{1,0:T(8,128)(2,1)S(1)} %multiply_convert_fusion.3, bf16[1024,2048]{1,0:T(8,128)(2,1)} %all-gather.9.cloned.1.call-done, f32[1024]{0:T(1024)S(1)} %bitcast_convert_fusion), kind=kOutput, calls=%fused_computation.16 | convolution fusion | flops 3229089792 | bytes 8916992 | tf_op jit(solution)/shard_map/dot_general | solution.py:25
  258.4 9.7 %multiply_convert_fusion.2 = (bf16[1024,768]{1,0:T(8,128)(2,1)S(1)}, bf16[1024,768]{1,0:T(8,128)(2,1)S(1)}) fusion(f32[1024,1536]{1,0:T(8,128)} %copy-done.1, bf16[1,768,2048]{2,1,0:T(8,128)(2,1)} %all-gather.13.cloned.1.call-done, bf16[1024,2048]{1,0:T(8,128)(2,1)} %all-gather.9.cloned.1.call-done, f32[1024]{0:T(1024)S(1)} %bitcast_convert_fusion), kind=kOutput, calls=%fused_computation.30 | convolution fusion | flops 3237740544 | bytes 16781312 | tf_op jit(solution)/shard_map/dot_general | solution.py:25
  268.1 8.8 %fusion.2 = bf16[2048,1536]{0,1:T(8,128)(2,1)} fusion(bf16[1024,2048]{1,0:T(8,128)(2,1)S(1)} %copy-done.5, bf16[1024,768]{1,0:T(8,128)(2,1)S(1)} %get-tuple-element.45, bf16[1024,768]{1,0:T(8,128)(2,1)S(1)} %get-tuple-element.44), kind=kOutput, calls=%fused_computation.6 | convolution fusion | flops 6451888128 | bytes 13631488 | tf_op jit(solution)/shard_map/dot_general | solution.py:25
  276.9 11.1 %fusion.7 = bf16[1024,2048]{1,0:T(8,128)(2,1)} fusion(bf16[1,2048,1536]{2,1,0:T(8,128)(2,1)} %all-gather.11.cloned.1.call-done, bf16[1024,768]{1,0:T(8,128)(2,1)S(1)} %get-tuple-element.45, bf16[1024,768]{1,0:T(8,128)(2,1)S(1)} %get-tuple-element.44), kind=kOutput, calls=%fused_computation.15 | convolution fusion | flops 6450839552 | bytes 13631488 | tf_op jit(solution)/shard_map/dot_general | solution.py:25
  288.3 6.0 %multiply_convert_fusion = bf16[1024,2048]{1,0:T(8,128)(2,1)} fusion(f32[1024,2048]{1,0:T(8,128)} %get-tuple-element.51, f32[1024]{0:T(1024)S(1)} %bitcast_convert_fusion), kind=kLoop, calls=%fused_computation.4 | loop fusion | flops 4194304 | bytes 12587008 | tf_op jit(solution)/shard_map/convert_element_type | solution.py:53
  294.3 1.4 copy-done
  295.7 1.6 copy.64
  297.3 2.4 copy.65
  299.7 0.7 reduce-scatter.11.cloned.1.call-done
  300.4 4.1 fusion.30
  304.5 69.0 %reduce-scatter.9.cloned.1.call-done = bf16[512,1536]{0,1:T(8,128)(2,1)} async-done(((bf16[2048,1536]{0,1:T(8,128)(2,1)}), bf16[512,1536]{0,1:T(8,128)(2,1)}) %reduce-scatter.9.cloned.1.call-update) | async-done | bytes 1572880 | tf_op jit(solution)/shard_map/reduce_scatter | solution.py:63
  373.5 5.8 %fusion.16 = (f32[1,512,1536]{1,2,0:T(8,128)}, bf16[1,512,1536]{1,2,0:T(8,128)(2,1)}) fusion(bf16[512,1536]{0,1:T(8,128)(2,1)} %reduce-scatter.9.cloned.1.call-done, f32[1,512,1536]{1,2,0:T(8,128)S(1)} %copy.65, bf16[1,512,1536]{1,2,0:T(8,128)(2,1)} %copy.64), kind=kLoop, calls=%fused_computation.23 | loop fusion | flops 12582912 | bytes 11010048 | tf_op jit(solution)/shard_map/add | solution.py:20
  379.2 3.7 copy.68
  382.9 1.6 copy.67
  384.5 41.9 %reduce-scatter.7.cloned.1.call-done = bf16[128,2048]{1,0:T(8,128)(2,1)} async-done(((bf16[1024,2048]{1,0:T(8,128)(2,1)}), bf16[128,2048]{1,0:T(8,128)(2,1)}) %reduce-scatter.7.cloned.1.call-update) | async-done | bytes 524304 | tf_op jit(solution)/shard_map/reduce_scatter | solution.py:65
  426.4 51.0 %reduce-scatter.5.cloned.1.call-done = bf16[128,2048]{1,0:T(8,128)(2,1)} async-done(((bf16[1024,2048]{1,0:T(8,128)(2,1)}), bf16[128,2048]{1,0:T(8,128)(2,1)}) %reduce-scatter.5.cloned.1.call-update) | async-done | bytes 524304 | tf_op jit(solution)/shard_map/reduce_scatter | solution.py:55
  (27 shorter events, 1.3 us)
Async XLA Ops:
  7.2 52.3 %all-gather.7.cloned.1.call-start = ((), (), s32[]{:S(2)}) async-start(), calls=%async_computation.6 | async-start | bytes 4718592 | tf_op jit(solution)/shard_map/all_gather | solution.py:32
  7.9 122.3 %all-gather.11.cloned.1.call-start = ((), (), s32[]{:S(2)}) async-start(), calls=%async_computation.12 | async-start | bytes 7864320 | tf_op jit(solution)/shard_map/all_gather | solution.py:40
  8.6 167.4 %all-gather.13.cloned.1.call-start = ((), (), s32[]{:S(2)}) async-start(), calls=%async_computation.13 | async-start | bytes 3932160 | tf_op jit(solution)/shard_map/all_gather | solution.py:41
  9.4 215.3 %all-gather.9.cloned.1.call-start = ((), (), s32[]{:S(2)}) async-start(), calls=%async_computation.8 | async-start | bytes 4718592 | tf_op jit(solution)/shard_map/all_gather | solution.py:33
  140.2 2.6 copy-start.1
  143.7 93.2 %copy-start.4 = (bf16[128,4]{0,1:T(4,128)(2,1)S(1)}, bf16[128,4]{0,1:T(4,128)(2,1)}, u32[]{:S(2)}) copy-start(bf16[128,4]{0,1:T(4,128)(2,1)} %param.11) | copy-start | bytes 3076
  143.7 98.6 %copy-start.3 = (s32[128,4]{0,1:T(4,128)S(1)}, s32[128,4]{0,1:T(4,128)}, u32[]{:S(2)}) copy-start(s32[128,4]{0,1:T(4,128)} %param.10) | copy-start | bytes 6148
  233.5 8.7 %all-to-all-start.1 = ((bf16[8,1,128]{2,1,0:T(2,128)(2,1)}), bf16[8,1,128]{2,1,0:T(2,128)(2,1)S(1)}, u32[]{:S(2)}, u32[]{:S(2)}) async-start(bf16[8,1,128]{2,1,0:T(2,128)(2,1)} %copy.63), calls=%async_computation.3 | async-start | bytes 8192 | tf_op jit(solution)/shard_map/all_to_all | solution.py:56
  236.9 63.6 %reduce-scatter.11.cloned.1.call-start = ((), (), s32[]{:S(2)}) async-start(), calls=%async_computation.11 | async-start | bytes 3932160 | tf_op jit(solution)/shard_map/reduce_scatter | solution.py:51
  258.1 115.3 %reduce-scatter.9.cloned.1.call-start = ((), (), s32[]{:S(2)}) async-start(), calls=%async_computation.10 | async-start | bytes 7864320 | tf_op jit(solution)/shard_map/reduce_scatter | solution.py:63
  258.4 9.7 %copy-start.5 = (bf16[1024,2048]{1,0:T(8,128)(2,1)S(1)}, bf16[1024,2048]{1,0:T(8,128)(2,1)}, u32[]{:S(2)}) copy-start(bf16[1024,2048]{1,0:T(8,128)(2,1)} %all-gather.7.cloned.1.call-done) | copy-start | bytes 12582916
  276.9 149.5 %reduce-scatter.7.cloned.1.call-start = ((), (), s32[]{:S(2)}) async-start(), calls=%async_computation.9 | async-start | bytes 4718592 | tf_op jit(solution)/shard_map/reduce_scatter | solution.py:65
  288.1 189.3 %reduce-scatter.5.cloned.1.call-start = ((), (), s32[]{:S(2)}) async-start(), calls=%async_computation.7 | async-start | bytes 4718592 | tf_op jit(solution)/shard_map/reduce_scatter | solution.py:55
  294.3 1.4 copy-start
  379.2 3.7 copy-start.2
Sparse Core Ops, SparseCore 0:
  9.6 49.8 all-gather.6
  61.3 68.8 all-gather.10
  132.1 43.9 all-gather.12
  177.5 47.1 all-gather.8
  258.3 42.1 reduce-scatter.10
  303.3 70.1 reduce-scatter.8
  376.3 50.0 reduce-scatter.6
  429.2 48.1 reduce-scatter.4

commit v2 on v1

--- a/solution.py
+++ b/solution.py
@@ -1,6 +1,10 @@
+import functools
+
 import jax
 import jax.numpy as jnp
 from jax import lax
+from jax.experimental import pallas as pl
+from jax.experimental.pallas import tpu as pltpu
 from jax.sharding import PartitionSpec as P
 
 FF = 768
@@ -71,9 +75,465 @@
     return (layer_out, tokens_grad, gate_grad, w_in_new, w_out_new, mom_in_new, mom_out_new)
 
 
+def fused_kernel(nz, tok_hbm, cot_hbm, gates_hbm, win_hbm, wout_hbm,
+                 layer_ref, tokg_ref, sg_ref, gin_ref, gout_ref,
+                 rows, cots, gall, win, wout, ab, hid, hg, wt, pr, up, dn, tin, tout,
+                 gi1, gi2, go1, go2, sgs, sgr,
+                 loc_sem, ch_send, ch_recv, pt_send, pt_recv, g_send, g_recv,
+                 w_send, w_recv, pr_send, pr_recv, rs_send, rs_recv, sg_send, sg_recv,
+                 gr_send, gr_recv):
+    f32, bf16 = jnp.float32, jnp.bfloat16
+    d, e = lax.axis_index("dp"), lax.axis_index("expert")
+    z, c = e // 2, e % 2
+    ne = 2 * nz
+    T = tok_hbm.shape[0]
+    D = tok_hbm.shape[1]
+    DI, FO = win_hbm.shape[0], wout_hbm.shape[0]
+    nb_x, nb_y, nb_g = d + 1 - 2 * (d % 2), (d + 2) % 4, 3 - d
+    partner = e + 1 - 2 * c
+    above, below = (d, e + 2), (d, e - 2)
+
+    def blk(index):
+        return pl.ds(pl.multiple_of(index * T, T), T)
+
+    def remote(src, dst, send, recv, dev):
+        return pltpu.make_async_remote_copy(
+            src_ref=src, dst_ref=dst, send_sem=send, recv_sem=recv,
+            device_id=dev, device_id_type=pl.DeviceIdType.MESH)
+
+    barrier = pltpu.get_barrier_semaphore()
+    for k in range(1, ne):
+        pl.semaphore_signal(barrier, inc=1, device_id=(d, (e + k) % ne),
+                            device_id_type=pl.DeviceIdType.MESH)
+    for nb in (nb_x, nb_y):
+        pl.semaphore_signal(barrier, inc=1, device_id=(nb, e),
+                            device_id_type=pl.DeviceIdType.MESH)
+
+    locs = [
+        pltpu.make_async_copy(tok_hbm, rows.at[blk(e)], loc_sem.at[0]),
+        pltpu.make_async_copy(win_hbm, win.at[pl.ds(pl.multiple_of(d * DI, DI), DI)], loc_sem.at[1]),
+        pltpu.make_async_copy(gates_hbm, gall.at[blk(e)], loc_sem.at[2]),
+        pltpu.make_async_copy(cot_hbm, cots.at[blk(e)], loc_sem.at[3]),
+        pltpu.make_async_copy(wout_hbm, wout.at[pl.ds(pl.multiple_of(d * FO, FO), FO)], loc_sem.at[4]),
+    ]
+    for cp in locs:
+        cp.start()
+    pl.semaphore_wait(barrier, ne + 1)
+
+    def ag_copy(a, index, way, s):
+        ref = (rows, cots)[a].at[blk(index)]
+        dev = above if way == 0 else below
+        return remote(ref, ref, ch_send.at[a, way, s], ch_recv.at[a, way, s], dev)
+
+    def pt_copy(a, index, s):
+        ref = (rows, cots)[a].at[blk(index)]
+        return remote(ref, ref, pt_send.at[a, s], pt_recv.at[a, s], (d, partner))
+
+    def ag_first(a):
+        @pl.when(z < nz - 1)
+        def _():
+            ag_copy(a, e, 0, 0).start()
+
+        @pl.when(z > 0)
+        def _():
+            ag_copy(a, e, 1, 0).start()
+
+        pt_copy(a, e, 0).start()
+
+    def ag_step(a, s):
+        @pl.when(z >= s)
+        def _():
+            ag_copy(a, e - 2 * s, 0, s - 1).wait_recv()
+            if s < nz - 1:
+                @pl.when(z < nz - 1)
+                def _():
+                    ag_copy(a, e - 2 * s, 0, s).start()
+            pt_copy(a, e - 2 * s, s).start()
+
+        @pl.when(z + s <= nz - 1)
+        def _():
+            ag_copy(a, e + 2 * s, 1, s - 1).wait_recv()
+            if s < nz - 1:
+                @pl.when(z > 0)
+                def _():
+                    ag_copy(a, e + 2 * s, 1, s).start()
+            pt_copy(a, e + 2 * s, nz - 1 + s).start()
+
+    def ag_end(a):
+        pt_copy(a, partner, 0).wait_recv()
+        pt_copy(a, e, 0).wait_send()
+        for s in range(1, nz):
+            @pl.when(z >= s)
+            def _():
+                pt_copy(a, partner - 2 * s, s).wait_recv()
+                pt_copy(a, e - 2 * s, s).wait_send()
+
+            @pl.when(z + s <= nz - 1)
+            def _():
+                pt_copy(a, partner + 2 * s, nz - 1 + s).wait_recv()
+                pt_copy(a, e + 2 * s, nz - 1 + s).wait_send()
+        for s in range(nz - 1):
+            @pl.when((z >= s) & (z < nz - 1))
+            def _():
+                ag_copy(a, e - 2 * s, 0, s).wait_send()
+
+            @pl.when((z + s <= nz - 1) & (z > 0))
+            def _():
+                ag_copy(a, e + 2 * s, 1, s).wait_send()
+
+    def w_copy(a, way, s, owner, half):
+        ref, n = ((win, DI), (wout, FO))[a]
+        part = ref.at[pl.ds(pl.multiple_of(owner * n + half * (n // 2), n // 2), n // 2)]
+        return remote(part, part, w_send.at[a, way, s], w_recv.at[a, way, s],
+                      ((nb_x, e), (nb_y, e))[way])
+
+    def w_first(a):
+        w_copy(a, 0, 0, d, 1).start()
+        w_copy(a, 1, 0, d, 0).start()
+        w_copy(a, 0, 1, d, 0).start()
+        w_copy(a, 1, 1, d, 1).start()
+
+    def w_forward(a):
+        w_copy(a, 0, 0, nb_x, 1).wait_recv()
+        w_copy(a, 1, 2, nb_x, 1).start()
+        w_copy(a, 1, 0, nb_y, 0).wait_recv()
+        w_copy(a, 0, 2, nb_y, 0).start()
+
+    def w_end(a):
+        w_copy(a, 0, 1, nb_x, 0).wait_recv()
+        w_copy(a, 1, 1, nb_y, 1).wait_recv()
+        w_copy(a, 0, 2, nb_g, 0).wait_recv()
+        w_copy(a, 1, 2, nb_g, 1).wait_recv()
+        for way, s, owner, half in ((0, 0, d, 1), (1, 0, d, 0), (0, 1, d, 0), (1, 1, d, 1),
+                                    (0, 2, nb_y, 0), (1, 2, nb_x, 1)):
+            w_copy(a, way, s, owner, half).wait_send()
+
+    def g_copy(k, index, dev):
+        ref = gall.at[blk(index)]
+        return remote(ref, ref, g_send.at[k - 1], g_recv.at[k - 1], (d, dev))
+
+    locs[0].wait()
+    ag_first(0)
+    locs[1].wait()
+    w_first(0)
+    locs[2].wait()
+    for k in range(1, ne):
+        g_copy(k, e, (e + k) % ne).start()
+    locs[3].wait()
+    ag_first(1)
+    locs[4].wait()
+    w_first(1)
+    ag_step(0, 1)
+    w_forward(0)
+    ag_step(1, 1)
+    ag_step(0, 2)
+    ag_step(0, 3)
+    for k in range(1, ne):
+        g_copy(k, (e + ne - k) % ne, (e + k) % ne).wait_recv()
+        g_copy(k, e, (e + k) % ne).wait_send()
+    ag_end(0)
+    w_end(0)
+    ag_step(1, 2)
+    w_forward(1)
+
+    def gate_of(r, n):
+        lane = lax.broadcasted_iota(jnp.int32, (n, 128), 1)
+        return jnp.sum(jnp.where(lane == e, gall[r, :].astype(f32), 0.0), axis=1, keepdims=True)
+
+    def mm(a, b, ca, cb):
+        return lax.dot_general(a, b, (((ca,), (cb,)), ((), ())), preferred_element_type=f32)
+
+    M1, N1 = 512, 256
+    col_steps = FF // N1
+    R = ne * T
+
+    def pre_step(i, carry):
+        r = pl.ds(pl.multiple_of((i // col_steps) * M1, M1), M1)
+        n = (i % col_steps) * N1
+        cg = pl.ds(pl.multiple_of(n, N1), N1)
+        cu = pl.ds(pl.multiple_of(n + FF, N1), N1)
+        x = rows[r, :]
+        gp = mm(x, win[:, cg], 1, 0)
+        upp = mm(x, win[:, cu], 1, 0)
+        sig = jax.nn.sigmoid(gp)
+        act = gp * sig
+        h = act * upp
+        hid[r, cg] = h.astype(bf16)
+        hg[r, cg] = (h * gate_of(r, M1)).astype(bf16)
+        ab[r, cg] = (upp * sig * (1.0 + gp * (1.0 - sig))).astype(bf16)
+        ab[r, cu] = act.astype(bf16)
+        return carry
+
+    lax.fori_loop(0, R // M1 * col_steps, pre_step, 0)
+    ag_step(1, 3)
+    ag_end(1)
+
+    def term_out_step(i, carry):
+        n = pl.ds(pl.multiple_of(i * 512, 512), 512)
+        tout[:, n] = mm(hg[...], cots[:, n], 0, 0).astype(bf16)
+        return carry
+
+    lax.fori_loop(0, D // 512, term_out_step, 0)
+
+    terms = ((tin, DI, gi1, gi2, gin_ref), (tout, FO, go1, go2, gout_ref))
+
+    def part(a, owner, half):
+        ref, n = terms[a][0], terms[a][1]
+        return ref.at[pl.ds(pl.multiple_of(owner * n + half * (n // 2), n // 2), n // 2)]
+
+    def gr_copy(a, way, s):
+        _, n, first, second, _ = terms[a]
+        h = n // 2
+        dev = ((nb_x, e), (nb_y, e))[way]
+        owner = (nb_x, nb_y)[way]
+        if s == 0:
+            src, dst = part(a, nb_g, 1 - way), first.at[way]
+        else:
+            half = (1 - way) if s == 1 else way
+            src, dst = part(a, owner, half), second.at[way, pl.ds(half * h, h)]
+        return remote(src, dst, gr_send.at[a, way, s], gr_recv.at[a, way, s], dev)
+
+    def gr_sum(a, way):
+        gr_copy(a, 1 - way, 0).wait_recv()
+        p = part(a, (nb_x, nb_y)[way], way)
+        p[...] = (p[...].astype(f32) + terms[a][2][1 - way].astype(f32)).astype(bf16)
+        gr_copy(a, way, 2).start()
+
+    def gr_end(a):
+        second, out = terms[a][3], terms[a][4]
+        h = terms[a][1] // 2
+        for half in range(2):
+            total = part(a, d, half)[...].astype(f32)
+            for way in range(2):
+                gr_copy(a, way, 1 if half == 1 - way else 2).wait_recv()
+                total = total + second[way, half * h:(half + 1) * h, :].astype(f32)
+            out[half * h:(half + 1) * h, :] = total.astype(bf16)
+        for way in range(2):
+            for s in range(3):
+                gr_copy(a, way, s).wait_send()
+
+    for way in range(2):
+        gr_copy(1, way, 0).start()
+    for way in range(2):
+        gr_copy(1, way, 1).start()
+
+    w_end(1)
+
+    def weighted_step(i, carry):
+        r = pl.ds(pl.multiple_of((i // 2) * 256, 256), 256)
+        n = pl.ds(pl.multiple_of((i % 2) * 1024, 1024), 1024)
+        wt[r, n] = mm(hg[r, :], wout[:, n], 1, 0).astype(bf16)
+        return carry
+
+    lax.fori_loop(0, R // 256 * 2, weighted_step, 0)
+
+    results = ((wt, layer_ref), (cots, tokg_ref))
+
+    def pr_copy(a, zz):
+        return remote(results[a][0].at[blk(2 * zz + 1 - c)], pr.at[a, zz],
+                      pr_send.at[a, zz], pr_recv.at[a, zz], (d, partner))
+
+    def pr_first(a):
+        for zz in range(nz):
+            pr_copy(a, zz).start()
+
+    def pr_end(a):
+        for zz in range(nz):
+            pr_copy(a, zz).wait()
+
+    def mine(a, b):
+        return results[a][0][blk(2 * b + c), :].astype(f32) + pr[a, b].astype(f32)
+
+    def rs_copy(a, way, k, src=None):
+        ref = (up, dn)[way]
+        src = ref.at[a, k % (nz - 1)] if src is None else src
+        return remote(src, ref.at[a, k - 1], rs_send.at[a, way, k - 1],
+                      rs_recv.at[a, way, k - 1], (above, below)[way])
+
+    def rs_step(a, k):
+        for way in range(2):
+            ref = (up, dn)[way]
+            has = (z + k <= nz - 1) if way == 0 else (z - k >= 0)
+            inner = (z > 0) if way == 0 else (z < nz - 1)
+            b = z + k if way == 0 else z - k
+            if k < nz - 1:
+                @pl.when(has & inner)
+                def _():
+                    rs_copy(a, way, k + 1).wait_recv()
+                    ref[a, k] = (mine(a, b) + ref[a, k].astype(f32)).astype(bf16)
+                    rs_copy(a, way, k).start()
+
+            @pl.when(has & jnp.logical_not(inner))
+            def _():
+                pr[a, b] = mine(a, b).astype(bf16)
+                rs_copy(a, way, k, pr.at[a, b]).start()
+
+    def rs_end(a):
+        out = results[a][1]
+
+        @pl.when(z == 0)
+        def _():
+            rs_copy(a, 1, 1).wait_recv()
+            out[...] = (mine(a, z) + dn[a, 0].astype(f32)).astype(bf16)
+
+        @pl.when(z == nz - 1)
+        def _():
+            rs_copy(a, 0, 1).wait_recv()
+            out[...] = (mine(a, z) + up[a, 0].astype(f32)).astype(bf16)
+
+        @pl.when((z > 0) & (z < nz - 1))
+        def _():
+            rs_copy(a, 1, 1).wait_recv()
+            rs_copy(a, 0, 1).wait_recv()
+            out[...] = (mine(a, z) + up[a, 0].astype(f32) + dn[a, 0].astype(f32)).astype(bf16)
+
+        for k in range(1, nz):
+            @pl.when(z + k <= nz - 1)
+            def _():
+                rs_copy(a, 0, k).wait_send()
+
+            @pl.when(z - k >= 0)
+            def _():
+                rs_copy(a, 1, k).wait_send()
+
+    pr_first(0)
+
+    def back_step(i, carry):
+        r = pl.ds(pl.multiple_of(i * 256, 256), 256)
+        q = mm(cots[r, :], wout[...], 1, 1)
+        sg = jnp.sum(hid[r, :].astype(f32) * q, axis=1, keepdims=True)
+        lane = lax.broadcasted_iota(jnp.int32, (256, 128), 1)
+        sgs[r, :] = jnp.where(lane == e, sg, 0.0)
+        gq = gate_of(r, 256) * q
+        ab[r, :FF] = (gq * ab[r, :FF].astype(f32)).astype(bf16)
+        ab[r, FF:] = (gq * ab[r, FF:].astype(f32)).astype(bf16)
+        return carry
+
+    lax.fori_loop(0, R // 256, back_step, 0)
+
+    def sg_copy(k):
+        to = (e + k) % ne
+        return remote(sgs.at[blk(to)], sgr.at[k - 1], sg_send.at[k - 1], sg_recv.at[k - 1], (d, to))
+
+    for k in range(1, ne):
+        sg_copy(k).start()
+    for way in range(2):
+        gr_sum(1, way)
+    pr_end(0)
+    rs_step(0, 3)
+
+    def term_in(i):
+        owner = jnp.where(i < 2, nb_g, jnp.where(i < 6, jnp.where(i % 2 == 0, nb_x, nb_y), d))
+        half = jnp.where((i == 2) | (i == 0) | (i == 5) | (i == 7), 1, 0)
+        h = DI // 2
+        at = pl.ds(pl.multiple_of(owner * DI + half * h, h), h)
+        tin[at, :] = mm(rows[:, at], ab[...], 0, 0).astype(bf16)
+
+    def slot_step(i, carry):
+        r = pl.ds(pl.multiple_of((i // 2) * 256, 256), 256)
+        n = pl.ds(pl.multiple_of((i % 2) * 1024, 1024), 1024)
+        cots[r, n] = mm(ab[r, :], win[n, :], 1, 1).astype(bf16)
+        return carry
+
+    def term_loop(lo, hi):
+        def step(i, carry):
+            term_in(i)
+            return carry
+
+        lax.fori_loop(lo, hi, step, 0)
+
+    term_loop(0, 4)
+    for s in range(2):
+        for way in range(2):
+            gr_copy(0, way, s).start()
+    rs_step(0, 2)
+    term_loop(4, 8)
+    lax.fori_loop(0, R // 256 * 2, slot_step, 0)
+    pr_first(1)
+    for way in range(2):
+        gr_sum(0, way)
+    rs_step(0, 1)
+    pr_end(1)
+    rs_step(1, 3)
+    rs_step(1, 2)
+    rs_end(0)
+    for k in range(1, ne):
+        sg_copy(k).wait()
+    acc = sgs[blk(e), :]
+    for k in range(1, ne):
+        acc = acc + sgr[k - 1]
+    sg_ref[...] = acc
+    gr_end(1)
+    rs_step(1, 1)
+    rs_end(1)
+    gr_end(0)
+
+
+def fused_call(nz, tokens, cotangent, gates, w_in, w_out):
+    bf16, f32 = jnp.bfloat16, jnp.float32
+    T, D = tokens.shape
+    DI, F2 = w_in.shape
+    FO = w_out.shape[0]
+    ne = 2 * nz
+    R = ne * T
+    dma = pltpu.SemaphoreType.DMA
+    return pl.pallas_call(
+        functools.partial(fused_kernel, nz),
+        out_shape=(
+            jax.ShapeDtypeStruct((T, D), bf16),
+            jax.ShapeDtypeStruct((T, D), bf16),
+            jax.ShapeDtypeStruct((T, 128), f32),
+            jax.ShapeDtypeStruct((DI, F2), bf16),
+            jax.ShapeDtypeStruct((FO, D), bf16),
+        ),
+        in_specs=[pl.BlockSpec(memory_space=pl.ANY)] * 5,
+        out_specs=tuple([pl.BlockSpec(memory_space=pltpu.VMEM)] * 5),
+        scratch_shapes=[
+            pltpu.VMEM((R, D), bf16), pltpu.VMEM((R, D), bf16), pltpu.VMEM((R, 128), bf16),
+            pltpu.VMEM((4 * DI, F2), bf16), pltpu.VMEM((4 * FO, D), bf16),
+            pltpu.VMEM((R, F2), bf16), pltpu.VMEM((R, FF), bf16), pltpu.VMEM((R, FF), bf16),
+            pltpu.VMEM((R, D), bf16),
+            pltpu.VMEM((2, nz, T, D), bf16), pltpu.VMEM((2, nz - 1, T, D), bf16),
+            pltpu.VMEM((2, nz - 1, T, D), bf16),
+            pltpu.VMEM((4 * DI, F2), bf16), pltpu.VMEM((4 * FO, D), bf16),
+            pltpu.VMEM((2, DI // 2, F2), bf16), pltpu.VMEM((2, DI, F2), bf16),
+            pltpu.VMEM((2, FO // 2, D), bf16), pltpu.VMEM((2, FO, D), bf16),
+            pltpu.VMEM((R, 128), f32), pltpu.VMEM((ne - 1, T, 128), f32),
+            dma((5,)), dma((2, 2, nz - 1)), dma((2, 2, nz - 1)),
+            dma((2, 2 * nz - 1)), dma((2, 2 * nz - 1)), dma((ne - 1,)), dma((ne - 1,)),
+            dma((2, 2, 3)), dma((2, 2, 3)), dma((2, nz)), dma((2, nz)),
+            dma((2, 2, nz - 1)), dma((2, 2, nz - 1)), dma((ne - 1,)), dma((ne - 1,)),
+            dma((2, 2, 3)), dma((2, 2, 3)),
+        ],
+        compiler_params=pltpu.CompilerParams(
+            collective_id=0, has_side_effects=True, vmem_limit_bytes=63 * 1024 * 1024),
+        cost_estimate=pl.CostEstimate(
+            flops=36 * R * D * FF, bytes_accessed=20 * 1024 * 1024, transcendentals=R * FF),
+    )(tokens, cotangent, gates, w_in, w_out)
+
+
+def fused_body(tokens, cotangent, expert_ids, gate_probs, w_in, w_out, mom_in, mom_out):
+    groups = lax.axis_size("expert")
+    hits = expert_ids[:, :, None] == jnp.arange(128, dtype=jnp.int32)[None, None, :]
+    gates = jnp.sum(
+        jnp.where(hits, gate_probs.astype(jnp.float32)[:, :, None], 0.0), axis=1
+    ).astype(jnp.bfloat16)
+    layer_out, tokens_grad, slot_gate, grad_in, grad_out = fused_call(
+        groups // 2, tokens, cotangent, gates, w_in[0], w_out[0]
+    )
+    gate_grad = jnp.sum(jnp.where(hits, slot_gate[:, None, :], 0.0), axis=2).astype(jnp.bfloat16)
+    w_in_new, mom_in_new = lion_update(w_in, mom_in, grad_in.astype(jnp.float32)[None])
+    w_out_new, mom_out_new = lion_update(w_out, mom_out, grad_out.astype(jnp.float32)[None])
+    return (layer_out, tokens_grad, gate_grad, w_in_new, w_out_new, mom_in_new, mom_out_new)
+
+
 def solution(mesh):
     rows_spec = P(("dp", "expert"), None)
     weight_spec = P("expert", "dp", None)
     in_specs = (rows_spec,) * 4 + (weight_spec,) * 4
     out_specs = (rows_spec,) * 3 + (weight_spec,) * 4
-    return jax.shard_map(body, mesh=mesh, in_specs=in_specs, out_specs=out_specs, check_vma=False)
+    fits = mesh.shape["dp"] == 4 and mesh.shape["expert"] == 8
+    return jax.shard_map(
+        fused_body if fits else body,
+        mesh=mesh, in_specs=in_specs, out_specs=out_specs, check_vma=False,
+    )

time: 485 us -> 206 us (0.42)
  waiting for transfers between devices: 372 us -> 0 us
  Pallas kernels: 0 us -> 191 us
  matrix products: 55.1 us -> 0 us
  between operations: 14.2 us -> 0.67 us
  local copies, waits for them, and re-layouts: 13.8 us -> 1.61 us
  blocking collectives: 7.91 us -> 0 us
    all_gather x4 -> x0, waiting for transfers between devices: 201 us -> none  [the longest x1 70.8 us: body(): full_in = lax.all_gather(w_in[0], 'dp', axis=0, tiled=True)]
    pallas_call x0 -> x1, Pallas kernels: none -> 191 us  [fused_call(): pl.pallas_call(functools.partial(fused_kernel, nz), out_shape=(jax.ShapeD...]
    reduce_scatter x4 -> x0, waiting for transfers between devices: 163 us -> none  [the longest x1 69 us: body(): grad_in = lax.psum_scatter(term_in, 'dp', scatter_dimension=0, tiled=True)]
    dot_general x6 -> x0, matrix products: 55.1 us -> none  [dot(): lax.dot_general(a, b, (contract, ((), ())), preferred_element_type=jnp.fl...]
    unnamed x16 -> x14, local copies, waits for them, and re-layouts: 13.2 us -> 1.61 us
    all_to_all x1 -> x0, blocking collectives: 7.91 us -> none  [body(): lax.all_to_all(gates.astype(jnp.bfloat16).T.reshape(groups, tok_rows), 'e...]
    convert_element_type x4 -> x1, other arithmetic: 6.84 us -> 0.68 us  [fused_body(): gate_probs.astype(jnp.float32)[:, :, None]]
    all_to_all x1 -> x0, waiting for transfers between devices: 5.34 us -> none  [body(): lax.all_to_all(slot_gate.reshape(groups, tok_rows), 'expert', 0, 0, tiled...]
  transfers between devices with their start and end apart: 9 -> 0, of which waited for: 9 -> 0; matrix products, arithmetic and copies ran while one was open for 14% -> 0% of each run, Pallas kernels for 0% -> 0%
where the time goes in v2:
time: 206 us
  Pallas kernels  191 us (93%)
  other arithmetic  12.9 us (6%)
    pallas_call x1, Pallas kernels, fused_call(): pl.pallas_call(functools.partial(fused_kernel, nz), out_shape=(jax.ShapeD...  191 us
    add x2, other arithmetic, lion_update(): new_moment = beta_two * moment + (1.0 - beta_two) * grad  9.09 us

profile of v2, /device:TPU:0, one launch (start us, length us, event | category | flops | bytes accessed | tf_op | source)
XLA Modules:
  0.0 205.8 jit_solution(5488456621216464950)
XLA Ops:
  0.6 0.7 convert_element_type.27
  1.3 1.5 select_reduce_fusion.1.gates_hbm
  2.8 0.0 copy-start.5
  2.8 190.6 %shard_map.135 = (bf16[128,2048]{1,0:T(8,128)(2,1)}, bf16[128,2048]{1,0:T(8,128)(2,1)}, f32[128,128]{1,0:T(8,128)}, bf16[512,1536]{1,0:T(8,128)(2,1)}, bf16[192,2048]{1,0:T(8,128)(2,1)}) custom-call(bf16[128,2048]{1,0:T(8,128)(2,1)} %tok_hbm.1, bf16[128,2048]{1,0:T(8,128)(2,1)} %cot_hbm.1, bf16[128,128]{1,0:T(8,128)(2,1)} %select_reduce_fusion.1.gates_hbm, ...), custom_call_target="tpu_custom_call" | custom-call | flops 57982058496 | bytes 20971520 | tf_op jit(solution)/shard_map/pallas_call | solution.py:480
  193.4 0.0 copy-done.5
  193.4 1.6 select_reduce_fusion
  195.0 0.0 copy-start
  195.0 0.0 copy-start.1
  195.1 0.0 copy-start.2
  195.1 6.9 %fusion.6 = (f32[1,512,1536]{2,1,0:T(8,128)}, bf16[1,512,1536]{2,1,0:T(8,128)(2,1)}) fusion(bf16[512,1536]{1,0:T(8,128)(2,1)} %get-tuple-element.15, f32[1,512,1536]{2,1,0:T(8,128)} %param.14, bf16[1,512,1536]{2,1,0:T(8,128)(2,1)} %param.12), kind=kLoop, calls=%fused_computation.10 | loop fusion | flops 12582912 | bytes 11010048 | tf_op jit(solution)/shard_map/add | solution.py:24
  201.9 0.0 copy-done
  201.9 0.0 copy-done.1
  201.9 0.0 copy-done.2
  201.9 0.0 copy-start.4
  201.9 0.0 copy-start.3
  201.9 2.2 %fusion.13 = (f32[1,192,2048]{2,1,0:T(8,128)}, bf16[1,192,2048]{2,1,0:T(8,128)(2,1)}) fusion(bf16[192,2048]{1,0:T(8,128)(2,1)S(1)} %copy-done.2, f32[1,192,2048]{2,1,0:T(8,128)S(1)} %copy-done, bf16[1,192,2048]{2,1,0:T(8,128)(2,1)S(1)} %copy-done.1), kind=kLoop, calls=%fused_computation.21 | loop fusion | flops 6291456 | bytes 5505024 | tf_op jit(solution)/shard_map/add | solution.py:24
  204.2 0.0 copy-done.4
  204.2 0.8 copy.19
  205.0 0.0 copy-done.3
  205.0 0.8 copy.20
Async XLA Ops:
  2.8 190.6 %copy-start.5 = (s32[128,4]{0,1:T(4,128)S(1)}, s32[128,4]{0,1:T(4,128)}, u32[]{:S(2)}) copy-start(s32[128,4]{0,1:T(4,128)} %param.10) | copy-start | bytes 6148
  195.0 6.9 %copy-start = (f32[1,192,2048]{2,1,0:T(8,128)S(1)}, f32[1,192,2048]{2,1,0:T(8,128)}, u32[]{:S(2)}) copy-start(f32[1,192,2048]{2,1,0:T(8,128)} %param.15) | copy-start | bytes 4718596
  195.0 6.9 %copy-start.1 = (bf16[1,192,2048]{2,1,0:T(8,128)(2,1)S(1)}, bf16[1,192,2048]{2,1,0:T(8,128)(2,1)}, u32[]{:S(2)}) copy-start(bf16[1,192,2048]{2,1,0:T(8,128)(2,1)} %param.13) | copy-start | bytes 2359300
  195.1 6.9 %copy-start.2 = (bf16[192,2048]{1,0:T(8,128)(2,1)S(1)}, bf16[192,2048]{1,0:T(8,128)(2,1)}, u32[]{:S(2)}) copy-start(bf16[192,2048]{1,0:T(8,128)(2,1)} %get-tuple-element.16) | copy-start | bytes 2359300
  201.9 2.3 %copy-start.4 = (bf16[128,2048]{1,0:T(8,128)(2,1)S(1)}, bf16[128,2048]{1,0:T(8,128)(2,1)}, u32[]{:S(2)}) copy-start(bf16[128,2048]{1,0:T(8,128)(2,1)} %get-tuple-element.28) | copy-start | bytes 1572868
  201.9 3.0 %copy-start.3 = (bf16[128,2048]{1,0:T(8,128)(2,1)S(1)}, bf16[128,2048]{1,0:T(8,128)(2,1)}, u32[]{:S(2)}) copy-start(bf16[128,2048]{1,0:T(8,128)(2,1)} %get-tuple-element.29) | copy-start | bytes 1572868

commit v3 on v2

--- a/solution.py
+++ b/solution.py
@@ -161,16 +161,24 @@
 
     def ag_end(a):
         pt_copy(a, partner, 0).wait_recv()
+        for s in range(1, nz):
+            @pl.when(z >= s)
+            def _():
+                pt_copy(a, partner - 2 * s, s).wait_recv()
+
+            @pl.when(z + s <= nz - 1)
+            def _():
+                pt_copy(a, partner + 2 * s, nz - 1 + s).wait_recv()
+
+    def ag_sent(a):
         pt_copy(a, e, 0).wait_send()
         for s in range(1, nz):
             @pl.when(z >= s)
             def _():
-                pt_copy(a, partner - 2 * s, s).wait_recv()
                 pt_copy(a, e - 2 * s, s).wait_send()
 
             @pl.when(z + s <= nz - 1)
             def _():
-                pt_copy(a, partner + 2 * s, nz - 1 + s).wait_recv()
                 pt_copy(a, e + 2 * s, nz - 1 + s).wait_send()
         for s in range(nz - 1):
             @pl.when((z >= s) & (z < nz - 1))
@@ -199,11 +207,15 @@
         w_copy(a, 1, 0, nb_y, 0).wait_recv()
         w_copy(a, 0, 2, nb_y, 0).start()
 
-    def w_end(a):
+    def w_middle(a):
         w_copy(a, 0, 1, nb_x, 0).wait_recv()
         w_copy(a, 1, 1, nb_y, 1).wait_recv()
+
+    def w_end(a):
         w_copy(a, 0, 2, nb_g, 0).wait_recv()
         w_copy(a, 1, 2, nb_g, 1).wait_recv()
+
+    def w_sent(a):
         for way, s, owner, half in ((0, 0, d, 1), (1, 0, d, 0), (0, 1, d, 0), (1, 1, d, 1),
                                     (0, 2, nb_y, 0), (1, 2, nb_x, 1)):
             w_copy(a, way, s, owner, half).wait_send()
@@ -220,21 +232,20 @@
     for k in range(1, ne):
         g_copy(k, e, (e + k) % ne).start()
     locs[3].wait()
-    ag_first(1)
     locs[4].wait()
-    w_first(1)
     ag_step(0, 1)
     w_forward(0)
-    ag_step(1, 1)
     ag_step(0, 2)
+    ag_first(1)
+    w_middle(0)
+    w_first(1)
     ag_step(0, 3)
     for k in range(1, ne):
         g_copy(k, (e + ne - k) % ne, (e + k) % ne).wait_recv()
         g_copy(k, e, (e + k) % ne).wait_send()
     ag_end(0)
+    ag_step(1, 1)
     w_end(0)
-    ag_step(1, 2)
-    w_forward(1)
 
     def gate_of(r, n):
         lane = lax.broadcasted_iota(jnp.int32, (n, 128), 1)
@@ -264,7 +275,12 @@
         ab[r, cu] = act.astype(bf16)
         return carry
 
-    lax.fori_loop(0, R // M1 * col_steps, pre_step, 0)
+    pre_steps = R // M1 * col_steps
+    lax.fori_loop(0, pre_steps // 3, pre_step, 0)
+    w_forward(1)
+    lax.fori_loop(pre_steps // 3, pre_steps * 2 // 3, pre_step, 0)
+    ag_step(1, 2)
+    lax.fori_loop(pre_steps * 2 // 3, pre_steps, pre_step, 0)
     ag_step(1, 3)
     ag_end(1)
 
@@ -317,6 +333,7 @@
     for way in range(2):
         gr_copy(1, way, 1).start()
 
+    w_middle(1)
     w_end(1)
 
     def weighted_step(i, carry):
@@ -446,16 +463,16 @@
     for s in range(2):
         for way in range(2):
             gr_copy(0, way, s).start()
+    term_loop(4, 8)
     rs_step(0, 2)
-    term_loop(4, 8)
+    ag_sent(1)
     lax.fori_loop(0, R // 256 * 2, slot_step, 0)
     pr_first(1)
-    for way in range(2):
-        gr_sum(0, way)
     rs_step(0, 1)
     pr_end(1)
     rs_step(1, 3)
-    rs_step(1, 2)
+    for way in range(2):
+        gr_sum(0, way)
     rs_end(0)
     for k in range(1, ne):
         sg_copy(k).wait()
@@ -463,9 +480,13 @@
     for k in range(1, ne):
         acc = acc + sgr[k - 1]
     sg_ref[...] = acc
+    rs_step(1, 2)
     gr_end(1)
     rs_step(1, 1)
     rs_end(1)
+    ag_sent(0)
+    w_sent(0)
+    w_sent(1)
     gr_end(0)
 
 

time: 206 us -> 197 us (0.956); the launches traced: 206 us -> 194 us
  Pallas kernels: 191 us -> 178 us
    pallas_call x1, Pallas kernels: 191 us -> 178 us  [fused_call(): pl.pallas_call(functools.partial(fused_kernel, nz), out_shape=(jax.ShapeD...]
where the time goes in v3:
time: 197 us; the launch traced here: 194 us
  Pallas kernels  178 us (90%)
  other arithmetic  12.9 us (7%)
    pallas_call x1, Pallas kernels, fused_call(): pl.pallas_call(functools.partial(fused_kernel, nz), out_shape=(jax.ShapeD...  178 us
    add x2, other arithmetic, lion_update(): new_moment = beta_two * moment + (1.0 - beta_two) * grad  9.09 us

profile of v3, /device:TPU:0, one launch (start us, length us, event | category | flops | bytes accessed | tf_op | source)
XLA Modules:
  0.0 193.5 jit_solution(7966552175639679614)
XLA Ops:
  0.6 0.7 convert_element_type.27
  1.3 1.5 select_reduce_fusion.1.gates_hbm
  2.8 0.0 copy-start.5
  2.8 178.3 %shard_map.135 = (bf16[128,2048]{1,0:T(8,128)(2,1)}, bf16[128,2048]{1,0:T(8,128)(2,1)}, f32[128,128]{1,0:T(8,128)}, bf16[512,1536]{1,0:T(8,128)(2,1)}, bf16[192,2048]{1,0:T(8,128)(2,1)}) custom-call(bf16[128,2048]{1,0:T(8,128)(2,1)} %tok_hbm.1, bf16[128,2048]{1,0:T(8,128)(2,1)} %cot_hbm.1, bf16[128,128]{1,0:T(8,128)(2,1)} %select_reduce_fusion.1.gates_hbm, ...), custom_call_target="tpu_custom_call" | custom-call | flops 57982058496 | bytes 20971520 | tf_op jit(solution)/shard_map/pallas_call | solution.py:501
  181.1 0.0 copy-done.5
  181.2 1.6 select_reduce_fusion
  182.8 0.0 copy-start
  182.8 0.0 copy-start.1
  182.8 0.0 copy-start.2
  182.8 6.9 %fusion.6 = (f32[1,512,1536]{2,1,0:T(8,128)}, bf16[1,512,1536]{2,1,0:T(8,128)(2,1)}) fusion(bf16[512,1536]{1,0:T(8,128)(2,1)} %get-tuple-element.15, f32[1,512,1536]{2,1,0:T(8,128)} %param.14, bf16[1,512,1536]{2,1,0:T(8,128)(2,1)} %param.12), kind=kLoop, calls=%fused_computation.10 | loop fusion | flops 12582912 | bytes 11010048 | tf_op jit(solution)/shard_map/add | solution.py:24
  189.7 0.0 copy-done
  189.7 0.0 copy-done.1
  189.7 0.0 copy-done.2
  189.7 0.0 copy-start.4
  189.7 0.0 copy-start.3
  189.7 2.2 %fusion.13 = (f32[1,192,2048]{2,1,0:T(8,128)}, bf16[1,192,2048]{2,1,0:T(8,128)(2,1)}) fusion(bf16[192,2048]{1,0:T(8,128)(2,1)S(1)} %copy-done.2, f32[1,192,2048]{2,1,0:T(8,128)S(1)} %copy-done, bf16[1,192,2048]{2,1,0:T(8,128)(2,1)S(1)} %copy-done.1), kind=kLoop, calls=%fused_computation.21 | loop fusion | flops 6291456 | bytes 5505024 | tf_op jit(solution)/shard_map/add | solution.py:24
  191.9 0.0 copy-done.4
  191.9 0.8 copy.19
  192.7 0.0 copy-done.3
  192.7 0.8 copy.20
Async XLA Ops:
  2.8 178.3 %copy-start.5 = (s32[128,4]{0,1:T(4,128)S(1)}, s32[128,4]{0,1:T(4,128)}, u32[]{:S(2)}) copy-start(s32[128,4]{0,1:T(4,128)} %param.10) | copy-start | bytes 6148
  182.8 6.9 %copy-start = (f32[1,192,2048]{2,1,0:T(8,128)S(1)}, f32[1,192,2048]{2,1,0:T(8,128)}, u32[]{:S(2)}) copy-start(f32[1,192,2048]{2,1,0:T(8,128)} %param.15) | copy-start | bytes 4718596
  182.8 6.9 %copy-start.1 = (bf16[1,192,2048]{2,1,0:T(8,128)(2,1)S(1)}, bf16[1,192,2048]{2,1,0:T(8,128)(2,1)}, u32[]{:S(2)}) copy-start(bf16[1,192,2048]{2,1,0:T(8,128)(2,1)} %param.13) | copy-start | bytes 2359300
  182.8 6.9 %copy-start.2 = (bf16[192,2048]{1,0:T(8,128)(2,1)S(1)}, bf16[192,2048]{1,0:T(8,128)(2,1)}, u32[]{:S(2)}) copy-start(bf16[192,2048]{1,0:T(8,128)(2,1)} %get-tuple-element.16) | copy-start | bytes 2359300
  189.7 2.3 %copy-start.4 = (bf16[128,2048]{1,0:T(8,128)(2,1)S(1)}, bf16[128,2048]{1,0:T(8,128)(2,1)}, u32[]{:S(2)}) copy-start(bf16[128,2048]{1,0:T(8,128)(2,1)} %get-tuple-element.28) | copy-start | bytes 1572868
  189.7 3.0 %copy-start.3 = (bf16[128,2048]{1,0:T(8,128)(2,1)S(1)}, bf16[128,2048]{1,0:T(8,128)(2,1)}, u32[]{:S(2)}) copy-start(bf16[128,2048]{1,0:T(8,128)(2,1)} %get-tuple-element.29) | copy-start | bytes 1572868

commit v4 on v3

--- a/solution.py
+++ b/solution.py
@@ -18,7 +18,7 @@
 
 def lion_update(weight, moment, grad):
     blend = beta_one * moment + (1.0 - beta_one) * grad
-    direction = blend / jnp.sqrt(blend * blend + 1.0)
+    direction = blend * lax.rsqrt(blend * blend + 1.0)
     wide = weight.astype(jnp.float32)
     new_weight = (wide - learn_rate * (direction + decay_rate * wide)).astype(jnp.bfloat16)
     new_moment = beta_two * moment + (1.0 - beta_two) * grad
@@ -75,7 +75,7 @@
     return (layer_out, tokens_grad, gate_grad, w_in_new, w_out_new, mom_in_new, mom_out_new)
 
 
-def fused_kernel(nz, tok_hbm, cot_hbm, gates_hbm, win_hbm, wout_hbm,
+def fused_kernel(nz, tok_hbm, cot_hbm, win_hbm, wout_hbm, ids_ref, probs_ref,
                  layer_ref, tokg_ref, sg_ref, gin_ref, gout_ref,
                  rows, cots, gall, win, wout, ab, hid, hg, wt, pr, up, dn, tin, tout,
                  gi1, gi2, go1, go2, sgs, sgr,
@@ -112,12 +112,17 @@
     locs = [
         pltpu.make_async_copy(tok_hbm, rows.at[blk(e)], loc_sem.at[0]),
         pltpu.make_async_copy(win_hbm, win.at[pl.ds(pl.multiple_of(d * DI, DI), DI)], loc_sem.at[1]),
-        pltpu.make_async_copy(gates_hbm, gall.at[blk(e)], loc_sem.at[2]),
-        pltpu.make_async_copy(cot_hbm, cots.at[blk(e)], loc_sem.at[3]),
-        pltpu.make_async_copy(wout_hbm, wout.at[pl.ds(pl.multiple_of(d * FO, FO), FO)], loc_sem.at[4]),
+        pltpu.make_async_copy(cot_hbm, cots.at[blk(e)], loc_sem.at[2]),
+        pltpu.make_async_copy(wout_hbm, wout.at[pl.ds(pl.multiple_of(d * FO, FO), FO)], loc_sem.at[3]),
     ]
     for cp in locs:
         cp.start()
+    lanes = lax.broadcasted_iota(jnp.int32, (T, 128), 1)
+    picks = [lanes == ids_ref[:, k:k + 1] for k in range(ids_ref.shape[1])]
+    dense = jnp.zeros((T, 128), f32)
+    for k, pick in enumerate(picks):
+        dense = jnp.where(pick, probs_ref[:, k:k + 1].astype(f32), dense)
+    gall[blk(e), :] = dense.astype(bf16)
     pl.semaphore_wait(barrier, ne + 1)
 
     def ag_copy(a, index, way, s):
@@ -228,11 +233,10 @@
     ag_first(0)
     locs[1].wait()
     w_first(0)
-    locs[2].wait()
     for k in range(1, ne):
         g_copy(k, e, (e + k) % ne).start()
+    locs[2].wait()
     locs[3].wait()
-    locs[4].wait()
     ag_step(0, 1)
     w_forward(0)
     ag_step(0, 2)
@@ -459,16 +463,21 @@
 
         lax.fori_loop(lo, hi, step, 0)
 
-    term_loop(0, 4)
-    for s in range(2):
-        for way in range(2):
-            gr_copy(0, way, s).start()
-    term_loop(4, 8)
+    term_loop(0, 2)
+    for way in range(2):
+        gr_copy(0, way, 0).start()
+    term_loop(2, 4)
+    for way in range(2):
+        gr_copy(0, way, 1).start()
+    term_loop(4, 6)
+    ag_sent(1)
+    slot_steps = R // 256 * 2
+    lax.fori_loop(0, slot_steps // 2, slot_step, 0)
     rs_step(0, 2)
-    ag_sent(1)
-    lax.fori_loop(0, R // 256 * 2, slot_step, 0)
+    lax.fori_loop(slot_steps // 2, slot_steps, slot_step, 0)
     pr_first(1)
     rs_step(0, 1)
+    term_loop(6, 8)
     pr_end(1)
     rs_step(1, 3)
     for way in range(2):
@@ -479,7 +488,13 @@
     acc = sgs[blk(e), :]
     for k in range(1, ne):
         acc = acc + sgr[k - 1]
-    sg_ref[...] = acc
+    top_lane = lax.broadcasted_iota(jnp.int32, (T, len(picks)), 1)
+    back = jnp.zeros((T, len(picks)), f32)
+    for k in range(len(picks)):
+        pick = lanes == ids_ref[:, k:k + 1]
+        value = jnp.sum(jnp.where(pick, acc, 0.0), axis=1, keepdims=True)
+        back = jnp.where(top_lane == k, value, back)
+    sg_ref[...] = back.astype(bf16)
     rs_step(1, 2)
     gr_end(1)
     rs_step(1, 1)
@@ -490,7 +505,7 @@
     gr_end(0)
 
 
-def fused_call(nz, tokens, cotangent, gates, w_in, w_out):
+def fused_call(nz, tokens, cotangent, w_in, w_out, expert_ids, gate_probs):
     bf16, f32 = jnp.bfloat16, jnp.float32
     T, D = tokens.shape
     DI, F2 = w_in.shape
@@ -503,11 +518,12 @@
         out_shape=(
             jax.ShapeDtypeStruct((T, D), bf16),
             jax.ShapeDtypeStruct((T, D), bf16),
-            jax.ShapeDtypeStruct((T, 128), f32),
+            jax.ShapeDtypeStruct(expert_ids.shape, bf16),
             jax.ShapeDtypeStruct((DI, F2), bf16),
             jax.ShapeDtypeStruct((FO, D), bf16),
         ),
-        in_specs=[pl.BlockSpec(memory_space=pl.ANY)] * 5,
+        in_specs=[pl.BlockSpec(memory_space=pl.ANY)] * 4
+        + [pl.BlockSpec(memory_space=pltpu.VMEM)] * 2,
         out_specs=tuple([pl.BlockSpec(memory_space=pltpu.VMEM)] * 5),
         scratch_shapes=[
             pltpu.VMEM((R, D), bf16), pltpu.VMEM((R, D), bf16), pltpu.VMEM((R, 128), bf16),
@@ -520,7 +536,7 @@
             pltpu.VMEM((2, DI // 2, F2), bf16), pltpu.VMEM((2, DI, F2), bf16),
             pltpu.VMEM((2, FO // 2, D), bf16), pltpu.VMEM((2, FO, D), bf16),
             pltpu.VMEM((R, 128), f32), pltpu.VMEM((ne - 1, T, 128), f32),
-            dma((5,)), dma((2, 2, nz - 1)), dma((2, 2, nz - 1)),
+            dma((4,)), dma((2, 2, nz - 1)), dma((2, 2, nz - 1)),
             dma((2, 2 * nz - 1)), dma((2, 2 * nz - 1)), dma((ne - 1,)), dma((ne - 1,)),
             dma((2, 2, 3)), dma((2, 2, 3)), dma((2, nz)), dma((2, nz)),
             dma((2, 2, nz - 1)), dma((2, 2, nz - 1)), dma((ne - 1,)), dma((ne - 1,)),
@@ -530,19 +546,14 @@
             collective_id=0, has_side_effects=True, vmem_limit_bytes=63 * 1024 * 1024),
         cost_estimate=pl.CostEstimate(
             flops=36 * R * D * FF, bytes_accessed=20 * 1024 * 1024, transcendentals=R * FF),
-    )(tokens, cotangent, gates, w_in, w_out)
+    )(tokens, cotangent, w_in, w_out, expert_ids, gate_probs)
 
 
 def fused_body(tokens, cotangent, expert_ids, gate_probs, w_in, w_out, mom_in, mom_out):
     groups = lax.axis_size("expert")
-    hits = expert_ids[:, :, None] == jnp.arange(128, dtype=jnp.int32)[None, None, :]
-    gates = jnp.sum(
-        jnp.where(hits, gate_probs.astype(jnp.float32)[:, :, None], 0.0), axis=1
-    ).astype(jnp.bfloat16)
-    layer_out, tokens_grad, slot_gate, grad_in, grad_out = fused_call(
-        groups // 2, tokens, cotangent, gates, w_in[0], w_out[0]
+    layer_out, tokens_grad, gate_grad, grad_in, grad_out = fused_call(
+        groups // 2, tokens, cotangent, w_in[0], w_out[0], expert_ids, gate_probs
     )
-    gate_grad = jnp.sum(jnp.where(hits, slot_gate[:, None, :], 0.0), axis=2).astype(jnp.bfloat16)
     w_in_new, mom_in_new = lion_update(w_in, mom_in, grad_in.astype(jnp.float32)[None])
     w_out_new, mom_out_new = lion_update(w_out, mom_out, grad_out.astype(jnp.float32)[None])
     return (layer_out, tokens_grad, gate_grad, w_in_new, w_out_new, mom_in_new, mom_out_new)

time: 197 us -> 198 us (level)
  local copies, waits for them, and re-layouts: 1.61 us -> 5.83 us
  other arithmetic: 12.9 us -> 9.09 us
    unnamed x14 -> x15, local copies, waits for them, and re-layouts: 1.61 us -> 5.83 us
    reduce_sum x2 -> x0, other arithmetic: 3.16 us -> none  [the longest x1 1.65 us: fused_body(): jnp.sum(jnp.where(hits, slot_gate[:, None, :], 0.0), axis=2)]
where the time goes in v4:
time: 198 us; the launch traced here: 195 us
  Pallas kernels  179 us (90%)
  other arithmetic  9.09 us (5%)
  local copies, waits for them, and re-layouts  5.83 us (3%)
    pallas_call x1, Pallas kernels, fused_call(): pl.pallas_call(functools.partial(fused_kernel, nz), out_shape=(jax.ShapeD...  179 us
    add x2, other arithmetic, lion_update(): new_moment = beta_two * moment + (1.0 - beta_two) * grad  9.09 us
    unnamed x15, local copies, waits for them, and re-layouts  5.83 us

profile of v4, /device:TPU:0, one launch (start us, length us, event | category | flops | bytes accessed | tf_op | source)
XLA Modules:
  0.0 194.6 jit_solution(764701910845539866)
XLA Ops:
  0.6 1.4 copy.15.ids_ref
  2.0 1.4 copy.16.probs_ref
  3.5 179.0 %shard_map.135 = (bf16[128,2048]{1,0:T(8,128)(2,1)}, bf16[128,2048]{1,0:T(8,128)(2,1)}, bf16[128,4]{1,0:T(8,128)(2,1)}, bf16[512,1536]{1,0:T(8,128)(2,1)}, bf16[192,2048]{1,0:T(8,128)(2,1)}) custom-call(bf16[128,2048]{1,0:T(8,128)(2,1)} %tok_hbm.1, bf16[128,2048]{1,0:T(8,128)(2,1)} %cot_hbm.1, bf16[512,1536]{1,0:T(8,128)(2,1)} %bitcast.22, ...), custom_call_target="tpu_custom_call" | custom-call | flops 57982058496 | bytes 20971520 | tf_op jit(solution)/shard_map/pallas_call | solution.py:516
  182.5 1.4 copy.17
  183.9 0.0 copy-start
  183.9 0.0 copy-start.1
  183.9 0.0 copy-start.2
  183.9 6.9 %fusion.6 = (f32[1,512,1536]{2,1,0:T(8,128)}, bf16[1,512,1536]{2,1,0:T(8,128)(2,1)}) fusion(bf16[512,1536]{1,0:T(8,128)(2,1)} %get-tuple-element.15, f32[1,512,1536]{2,1,0:T(8,128)} %param.14, bf16[1,512,1536]{2,1,0:T(8,128)(2,1)} %param.12), kind=kLoop, calls=%fused_computation.10 | loop fusion | flops 12582912 | bytes 11010048 | tf_op jit(solution)/shard_map/add | solution.py:24
  190.7 0.0 copy-done
  190.7 0.0 copy-done.1
  190.7 0.0 copy-done.2
  190.7 0.0 copy-start.4
  190.7 0.0 copy-start.3
  190.8 2.2 %fusion.13 = (f32[1,192,2048]{2,1,0:T(8,128)}, bf16[1,192,2048]{2,1,0:T(8,128)(2,1)}) fusion(bf16[192,2048]{1,0:T(8,128)(2,1)S(1)} %copy-done.2, f32[1,192,2048]{2,1,0:T(8,128)S(1)} %copy-done, bf16[1,192,2048]{2,1,0:T(8,128)(2,1)S(1)} %copy-done.1), kind=kLoop, calls=%fused_computation.21 | loop fusion | flops 6291456 | bytes 5505024 | tf_op jit(solution)/shard_map/add | solution.py:24
  193.0 0.0 copy-done.4
  193.0 0.8 copy.20
  193.8 0.0 copy-done.3
  193.8 0.8 copy.21
Async XLA Ops:
  183.9 6.9 %copy-start = (f32[1,192,2048]{2,1,0:T(8,128)S(1)}, f32[1,192,2048]{2,1,0:T(8,128)}, u32[]{:S(2)}) copy-start(f32[1,192,2048]{2,1,0:T(8,128)} %param.15) | copy-start | bytes 4718596
  183.9 6.9 %copy-start.1 = (bf16[1,192,2048]{2,1,0:T(8,128)(2,1)S(1)}, bf16[1,192,2048]{2,1,0:T(8,128)(2,1)}, u32[]{:S(2)}) copy-start(bf16[1,192,2048]{2,1,0:T(8,128)(2,1)} %param.13) | copy-start | bytes 2359300
  183.9 6.9 %copy-start.2 = (bf16[192,2048]{1,0:T(8,128)(2,1)S(1)}, bf16[192,2048]{1,0:T(8,128)(2,1)}, u32[]{:S(2)}) copy-start(bf16[192,2048]{1,0:T(8,128)(2,1)} %get-tuple-element.16) | copy-start | bytes 2359300
  190.7 2.3 %copy-start.4 = (bf16[128,2048]{1,0:T(8,128)(2,1)S(1)}, bf16[128,2048]{1,0:T(8,128)(2,1)}, u32[]{:S(2)}) copy-start(bf16[128,2048]{1,0:T(8,128)(2,1)} %get-tuple-element.35) | copy-start | bytes 1572868
  190.7 3.0 %copy-start.3 = (bf16[128,2048]{1,0:T(8,128)(2,1)S(1)}, bf16[128,2048]{1,0:T(8,128)(2,1)}, u32[]{:S(2)}) copy-start(bf16[128,2048]{1,0:T(8,128)(2,1)} %get-tuple-element.36) | copy-start | bytes 1572868
